TPU v7x, 256 devices: a whole 4x4x8 slice. The times are simulated.
256 devices in a mesh: front: 16 (over z, core), row: 4 (over x), col: 4 (over y).
Axes of the slice: x: 4, y: 4, z: 8, core: 2. Of those that a mesh axis runs over, the one named last changes fastest.
Arguments:
- front: float32 [4, 128, 128, 4, 8, 128], P('row', 'front', None, 'col'), parts along dimension 1, as said below
- pattern: int32 [32, 32, 32], P('front'), parts along dimension 0, may hold values from 0 to 1, as said below
Outputs:
- factored: float32 [4, 128, 128, 4, 8, 128], P('row', 'front', None, 'col'), parts along dimension 1
There are 16 independent parts, one for each index of `front`. A program takes and returns all parts, laid end to end along the dimension named above; each array names one. Nothing has to cross between parts.
Inputs may be any that keep to these rules, and one draw needn't show every extreme that they name: `pattern`: 0 or 1; symmetric in the two block indices; 1 on the block diagonal and on every block pair whose two block indices are both below 8. `front`: symmetric positive definite.
All inputs are finite; a program needn't handle non-finite values.
Results may differ from a plain program's by a relative error of at most 0.0001.
Values sent between devices are 32-bit elements; how exact they have to be, the bound alone decides.
No kernel may reach another device: no remote copies, remote signals or barrier semaphores. Data moves between devices by JAX's collectives and lax.ppermute only.
A program may use at most 128 MiB of HBM per device.

v0:
```python
import functools

import jax
import jax.numpy as jnp
from jax import lax
from jax.experimental import pallas as pl
from jax.experimental.pallas import tpu as pltpu
from jax.sharding import PartitionSpec as P

F32 = jnp.float32
BF16 = jnp.bfloat16
HI = lax.Precision.HIGHEST
EDGE = 128
TILE = 8
HALF = EDGE // 2
HELD = HALF + TILE
GROUPS = 4
WIDTH = EDGE * GROUPS
LB = 8
BATCH = 4
NPAN = 2
REST = LB - NPAN
ROWS = REST * EDGE

NN = (((1,), (0,)), ((), ()))
NT = (((1,), (1,)), ((), ()))
TN = (((0,), (0,)), ((), ()))


def exact_dot(a, b, dims):
    return lax.dot_general(a, b, dims, precision=HI, preferred_element_type=F32)


def split2(x):
    high = x.astype(BF16)
    return high, (x - high.astype(F32)).astype(BF16)


def split3(x):
    high = x.astype(BF16)
    rest = x - high.astype(F32)
    mid = rest.astype(BF16)
    return high, mid, (rest - mid.astype(F32)).astype(BF16)


def dot3(a, b, dims):
    one = functools.partial(lax.dot_general, dimension_numbers=dims, preferred_element_type=F32)
    return one(a[0], b[0]) + (one(a[0], b[1]) + one(a[1], b[0]))


def spread(x):
    return jnp.broadcast_to(x, (TILE, EDGE))


def factor_block(a, w):
    sub = lax.broadcasted_iota(jnp.int32, (TILE, EDGE), 0)
    count = EDGE // TILE
    left, right = a[:TILE, :], w[:TILE, :]
    for p in range(count):
        at, after = slice(TILE * p, TILE * (p + 1)), slice(TILE * (p + 1), TILE * (p + 2))
        more = p + 1 < count
        cols = [spread(left[:, TILE * p + q:TILE * p + q + 1]) for q in range(TILE)]
        if more:
            next_left, next_right = a[after, :], w[after, :]
            next_cols = [spread(next_left[:, TILE * p + q:TILE * p + q + 1]) for q in range(TILE)]
        invs = jnp.zeros((TILE, EDGE), F32)
        pivot = spread(cols[0][:1, :])
        for q in range(TILE):
            inv = 1.0 / pivot
            if q + 1 < TILE:
                beside = spread(cols[q + 1][q:q + 1, :])
                pivot = spread(cols[q + 1][q + 1:q + 2, :]) - (beside * beside) * inv
            m = jnp.where(sub > q, cols[q], 0.0) * inv
            invs = jnp.where(sub == q, inv, invs)
            row_left, row_right = spread(left[q:q + 1, :]), spread(right[q:q + 1, :])
            left, right = left - m * row_left, right - m * row_right
            if more:
                n = next_cols[q] * inv
                next_left, next_right = next_left - n * row_left, next_right - n * row_right
            for t in range(q + 1, TILE):
                across = spread(cols[t][q:q + 1, :])
                cols[t] = cols[t] - m * across
                if more:
                    next_cols[t] = next_cols[t] - n * across
        root = lax.rsqrt(invs) * invs
        left, right = left * root, right * root
        a[at, :], w[at, :] = left, right
        low = TILE * (p + 2)
        if low < EDGE:
            h, m, l = split3(left)
            vh, vm, vl = split3(right)
            uh, um, ul = (jnp.concatenate(pair, 1) for pair in ((h, vh), (m, vm), (l, vl)))
            lhs = jnp.concatenate([h, h, m, h, m, l], 0)
            rhs = jnp.concatenate([uh, um, uh, ul, um, uh], 0)
            change = lax.dot_general(lhs, rhs, TN, preferred_element_type=F32)
            a[low:, :] = a[low:, :] - change[low:, :EDGE]
            w[low:, :] = w[low:, :] - change[low:, EDGE:]
        if more:
            left, right = next_left, next_right


def factor_panel(s, lower, inverse, a, w):
    ri = lax.broadcasted_iota(jnp.int32, (EDGE, EDGE), 0)
    ci = lax.broadcasted_iota(jnp.int32, (EDGE, EDGE), 1)
    for k in range(GROUPS):
        here = slice(k * EDGE, (k + 1) * EDGE)
        below = slice((k + 1) * EDGE, WIDTH)
        before = slice(0, k * EDGE)
        a[k] = s[here, here]
        w[k] = jnp.where(ri == ci, 1.0, 0.0)
        factor_block(a.at[k], w.at[k])
        d = w[k]
        if k + 1 < GROUPS:
            part = exact_dot(s[below, here], d, NT)
            lower[below, here] = part
            s[below, below] = s[below, below] - exact_dot(part, part, NT)
            lower[here, below] = jnp.zeros((EDGE, WIDTH - (k + 1) * EDGE), F32)
            inverse[here, below] = jnp.zeros((EDGE, WIDTH - (k + 1) * EDGE), F32)
        lower[here, here] = jnp.where(ri <= ci, a[k], 0.0).T
        inverse[here, here] = d
        if k > 0:
            part = exact_dot(lower[here, before], inverse[before, before], NN)
            inverse[here, before] = -exact_dot(d, part, NN)


def pack(block, ref, r, c):
    row = lax.broadcasted_iota(jnp.int32, (HALF, EDGE), 0)
    lane = lax.broadcasted_iota(jnp.int32, (HALF, EDGE), 1)
    top, low = block[:HALF], block[HALF:]
    diagonal = jnp.where(lane - HALF > row, pltpu.roll(top, HALF, 1), low)
    ref[:HALF, :] = jnp.where(r == c, diagonal, jnp.where(r > c, top, block.T[HALF:]))
    ref[HALF:HELD, :] = spread(jnp.sum(jnp.where(lane == row, top, 0.0), axis=0, keepdims=True))


def unpack_diagonal(got):
    row = lax.broadcasted_iota(jnp.int32, (EDGE, EDGE), 0)
    lane = lax.broadcasted_iota(jnp.int32, (EDGE, EDGE), 1)
    body = got[:HALF]
    some = jnp.concatenate([pltpu.roll(body, HALF, 1), body], 0)
    kept = ((row >= HALF) & (lane <= row)) | ((lane < HALF) & (row < lane))
    whole = jnp.where(kept, some, some.T)
    return jnp.where((row == lane) & (row < HALF), jnp.broadcast_to(got[HALF:HALF + 1], (EDGE, EDGE)), whole)


def unpack(got, at, s):
    for r in range(GROUPS):
        for c in range(r):
            span = slice(c * EDGE, (c + 1) * EDGE)
            s[r * EDGE:r * EDGE + HALF, span] = got[r * GROUPS + c, at:at + HALF]
            s[r * EDGE + HALF:(r + 1) * EDGE, span] = got[c * GROUPS + r, at:at + HALF]
        span = slice(r * EDGE, (r + 1) * EDGE)
        s[span, span] = unpack_diagonal(got[r * GROUPS + r, at:at + HELD])


def first_kernel(got, lower, inverse, s, a, w):
    unpack(got, 0, s)
    factor_panel(s, lower, inverse, a, w)


def second_kernel(got, inverse0, across, lower, inverse, s, a, w):
    for r in range(GROUPS):
        for c in range(GROUPS):
            s[r * EDGE:(r + 1) * EDGE, c * EDGE:(c + 1) * EDGE] = got[r * GROUPS + c, :EDGE]
    across[...] = dot3(split2(s[...]), split2(inverse0[...]), NT)
    unpack(got, EDGE, s)
    part = split2(across[...])
    s[...] = s[...] - dot3(part, part, NT)
    factor_panel(s, lower, inverse, a, w)


def collect(ids, at, flags):
    for number, flag in flags:
        ids[at] = number
        at = at + jnp.where(flag, 1, 0)
    return at


def visit(ids, first, last, product, target):
    def step(i, _):
        slots = [first + i * BATCH + j for j in range(BATCH)]
        numbers = [ids[jnp.minimum(slot, last - 1)] for slot in slots]
        changes = [jnp.where(slot < last, product(number), 0.0) for slot, number in zip(slots, numbers)]
        for number, change in zip(numbers, changes):
            target(number, change)
        return 0

    lax.fori_loop(0, lax.div(last - first + BATCH - 1, BATCH), step, 0)


def spans(i):
    return pl.ds(pl.multiple_of(i * EDGE, EDGE), EDGE)


def last_kernel(front, pattern, ar, ac0, ac1, ac3, ac2, low0, inv0, across, low1, inv1, out,
                buf, arv, acv, xh, xl, yh, yl, th, tl, sh, sl, bh, bl, lr, lc, ids, arrive, leave):
    r, c = lax.axis_index("row"), lax.axis_index("col")
    own, mine = spans(c), spans(r)
    half = WIDTH // 2
    loads = []
    for k in range(NPAN):
        loads.append(pltpu.make_async_copy(ar.at[:, k], arv.at[:, k], arrive.at[8 * k]))
        for s, ac in ((0, ac0), (1, ac1), (2, ac2), (3, ac3)):
            loads.append(pltpu.make_async_copy(ac.at[k], acv.at[(r + GROUPS - s) % GROUPS, k], arrive.at[8 * k + s + 1]))
    fronts = [pltpu.make_async_copy(front.at[l], buf.at[l], arrive.at[16 + l]) for l in range(NPAN, LB)]
    for load in loads + fronts:
        load.start()
    zero = jnp.zeros((EDGE, EDGE), F32)
    for l in range(NPAN):
        for m in range(NPAN, LB):
            buf[l, :, m, :] = zero
    buf[0, :, 1, :] = zero
    buf[0, :, 0, :] = low0[mine, own]
    buf[1, :, 0, :] = across[mine, own]
    buf[1, :, 1, :] = low1[mine, own]
    stores = [pltpu.make_async_copy(buf.at[:NPAN], out.at[:NPAN], leave.at[0])]
    stores[0].start()
    bh[...], bl[...] = split2(across[...])
    side = [(l, g) for l in range(REST) for g in range(GROUPS)]
    row_end = collect(ids, 0, [
        (l * TILE + g, pattern[0, (l + NPAN) * GROUPS + r, GROUPS + g] > 0) for l, g in side])
    col_end = collect(ids, row_end, [
        (l * TILE + g, pattern[0, GROUPS + g, (l + NPAN) * GROUPS + c] > 0) for l, g in side])
    all_end = collect(ids, col_end, [
        ((k * TILE + l) * TILE + m, pattern[k, (l + NPAN) * GROUPS + r, (m + NPAN) * GROUPS + c] > 0)
        for k in range(NPAN) for l in range(REST) for m in range(REST)])

    def row_product(number):
        l, g = lax.div(number, TILE), lax.rem(number, TILE)
        return dot3((xh[0, spans(l), :], xl[0, spans(l), :]), (bh[spans(g), :], bl[spans(g), :]), NT)

    def row_target(number, change):
        l, g = lax.div(number, TILE), lax.rem(number, TILE)
        arv[g, 1, l] = arv[g, 1, l] - change

    def col_product(number):
        l, g = lax.div(number, TILE), lax.rem(number, TILE)
        return dot3((bh[spans(g), :], bl[spans(g), :]), (yh[0, :, spans(l)], yl[0, :, spans(l)]), NN)

    def col_target(number, change):
        l, g = lax.div(number, TILE), lax.rem(number, TILE)
        acv[g, 1, :, spans(l)] = acv[g, 1, :, spans(l)] - change

    def place(number):
        row = lax.div(number, TILE)
        return lax.div(row, TILE), lax.rem(row, TILE), lax.rem(number, TILE)

    def product(number):
        k, l, m = place(number)
        return dot3((xh[k, spans(l), :], xl[k, spans(l), :]), (yh[k, :, spans(m)], yl[k, :, spans(m)]), NN)

    def target(number, change):
        k, l, m = place(number)
        buf[l + NPAN, :, m + NPAN, :] = buf[l + NPAN, :, m + NPAN, :] - change

    for k in range(NPAN):
        for load in loads[5 * k:5 * k + 5]:
            load.wait()
        if k == 1:
            visit(ids, 0, row_end, row_product, row_target)
            visit(ids, row_end, col_end, col_product, col_target)
        for g in range(GROUPS):
            span = slice(g * EDGE, (g + 1) * EDGE)
            th[:, span], tl[:, span] = split2(arv[g, k].reshape(ROWS, EDGE))
            sh[span, :], sl[span, :] = split2(acv[g, k])
        wh, wl = split2((inv0, inv1)[k][...])
        lr[:, :half] = dot3((th[:, :half], tl[:, :half]), (wh[:half, :half], wl[:half, :half]), NT)
        lr[:, half:] = dot3((th[...], tl[...]), (wh[half:, :], wl[half:, :]), NT)
        xh[k], xl[k] = split2(lr[...])
        lc[:half, :] = dot3((wh[:half, :half], wl[:half, :half]), (sh[:half, :], sl[:half, :]), NN)
        lc[half:, :] = dot3((wh[half:, :], wl[half:, :]), (sh[...], sl[...]), NN)
        yh[k], yl[k] = split2(lc[...])
        if k == 0:
            for load in fronts:
                load.wait()
        for l in range(REST):
            buf[l + NPAN, :, k, :] = lr[l * EDGE:(l + 1) * EDGE, own]
    visit(ids, col_end, all_end, product, target)
    stores.append(pltpu.make_async_copy(buf.at[NPAN:], out.at[NPAN:], leave.at[1]))
    stores[-1].start()
    for store in stores:
        store.wait()


def run(copies):
    for copy in copies:
        copy.start()
    for copy in copies:
        copy.wait()


def extract_kernel(front, ar, ac, rows, cols, sem):
    copy = pltpu.make_async_copy
    loads = [copy(front.at[NPAN:, :, k, :], rows.at[k], sem.at[k]) for k in range(NPAN)]
    for k in range(NPAN):
        for j in range(REST):
            loads.append(copy(front.at[k, :, j + NPAN, :], cols.at[k, :, j * EDGE:(j + 1) * EDGE], sem.at[len(loads)]))
    run(loads)
    run([copy(rows, ar, sem.at[0]), copy(cols, ac, sem.at[1])])


def corner_kernel(front, c0, c1, first, second, third, send0, send1, sem):
    r, c = lax.axis_index("row"), lax.axis_index("col")
    copy = pltpu.make_async_copy
    every = GROUPS * GROUPS
    loads = [copy(front.at[l, :, m, :], to, sem.at[i])
             for i, (l, m, to) in enumerate(((0, 0, first), (1, 0, send1.at[:EDGE]), (1, 1, third)))]
    for one in loads:
        one.start()
    loads[0].wait()
    pack(first[...], send0, r, c)
    stores = [copy(send0, c0.at[g], sem.at[3 + g]) for g in range(every)]
    for one in stores:
        one.start()
    loads[1].wait()
    loads[2].wait()
    pack(third[...], second, r, c)
    send1[EDGE:, :] = second[...]
    last = [copy(send1, c1.at[g], sem.at[3 + every + g]) for g in range(every)]
    for one in last:
        one.start()
    for one in stores + last:
        one.wait()


def shape(*dims):
    return jax.ShapeDtypeStruct(dims, F32)


def vmem(*dims, dtype=F32):
    return pltpu.VMEM(dims, dtype)


def call(kernel, outs, scratch=(), limit=60, **kw):
    return pl.pallas_call(
        kernel, out_shape=outs, scratch_shapes=list(scratch),
        compiler_params=pltpu.CompilerParams(vmem_limit_bytes=limit * 1024 * 1024), **kw)


def per_device(front, pattern):
    blocks = front[0, :, :, 0]
    work = [vmem(WIDTH, WIDTH), vmem(GROUPS, EDGE, EDGE), vmem(GROUPS, EDGE, EDGE)]
    square = shape(WIDTH, WIDTH)
    every = GROUPS * GROUPS
    away, dma = pl.BlockSpec(memory_space=pltpu.HBM), pltpu.SemaphoreType.DMA
    c0, c1 = call(
        corner_kernel, [shape(every, HELD, EDGE), shape(every, EDGE + HELD, EDGE)],
        [vmem(EDGE, EDGE), vmem(HELD, EDGE), vmem(EDGE, EDGE), vmem(HELD, EDGE), vmem(EDGE + HELD, EDGE), dma((3 + 2 * every,))],
        in_specs=[away], out_specs=[away, away],
    )(blocks)
    later, c0 = lax.optimization_barrier((blocks, c0))
    got0 = lax.all_to_all(c0, ("row", "col"), 0, 0, tiled=True)
    ar, ac = call(
        extract_kernel, [shape(NPAN, REST, EDGE, EDGE), shape(NPAN, EDGE, ROWS)],
        [vmem(NPAN, REST, EDGE, EDGE), vmem(NPAN, EDGE, ROWS), dma((NPAN + NPAN * REST,))],
        in_specs=[away], out_specs=[away, away],
    )(later)
    ar = lax.all_gather(ar, "col", axis=0)
    c1, got0 = lax.optimization_barrier((c1, got0))
    got1 = lax.all_to_all(c1, ("row", "col"), 0, 0, tiled=True)
    low0, inv0 = call(first_kernel, [square] * 2, work)(got0)
    ac, got1, inv0 = lax.optimization_barrier((ac, got1, inv0))
    acs = [ac] + [lax.ppermute(ac, "row", [(i, (i + s) % GROUPS) for i in range(GROUPS)]) for s in (1, 3, 2)]
    across, low1, inv1 = call(second_kernel, [square] * 3, work)(got1, inv0)
    whole = pl.BlockSpec(memory_space=pltpu.VMEM)
    result = call(
        last_kernel, shape(LB, EDGE, LB, EDGE),
        [vmem(LB, EDGE, LB, EDGE), vmem(GROUPS, NPAN, REST, EDGE, EDGE), vmem(GROUPS, NPAN, EDGE, ROWS)]
        + [vmem(NPAN, ROWS, WIDTH, dtype=BF16)] * 2 + [vmem(NPAN, WIDTH, ROWS, dtype=BF16)] * 2 + [vmem(ROWS, WIDTH, dtype=BF16)] * 2
        + [vmem(WIDTH, ROWS, dtype=BF16)] * 2 + [vmem(WIDTH, WIDTH, dtype=BF16)] * 2
        + [vmem(ROWS, WIDTH), vmem(WIDTH, ROWS), pltpu.SMEM((128,), jnp.int32), dma((24,)), dma((2,))],
        in_specs=[away, pl.BlockSpec(memory_space=pltpu.SMEM), away, away, away, away, away] + [whole] * 5,
        out_specs=away,
    )(blocks, pattern, ar, *acs, low0, inv0, across, low1, inv1)
    return result[None, :, :, None]


def solution(mesh):
    placed = (P("row", "front", None, "col", None, None), P("front", None, None))
    return jax.shard_map(
        per_device, mesh=mesh, in_specs=placed,
        out_specs=P("row", "front", None, "col", None, None), check_vma=False,
    )
```

profile of v0, /device:TPU:213, one launch (start us, length us, event | category | flops | bytes accessed | tf_op | source)
XLA Modules:
  0.0 120.7 jit_solution(4829389685524992847)
XLA Ops:
  6.5 0.0 all-gather.3.cloned.1.call-start
  6.5 2.6 %shard_map.28 = (f32[16,72,128]{2,1,0:T(8,128)}, f32[16,200,128]{2,1,0:T(8,128)}) custom-call(f32[8,128,8,128]{3,2,1,0:T(8,128)} %bitcast.5), custom_call_target="tpu_custom_call" | custom-call | tf_op jit(solution)/shard_map/pallas_call | solution.py:345
  9.2 0.0 copy-start.3
  9.2 2.7 %shard_map.29 = (f32[2,6,128,128]{3,2,1,0:T(8,128)}, f32[2,128,768]{2,1,0:T(8,128)}) custom-call(f32[8,128,8,128]{3,2,1,0:T(8,128)} %bitcast.6), custom_call_target="tpu_custom_call" | custom-call | tf_op jit(solution)/shard_map/pallas_call | solution.py:352
  11.9 0.0 copy-start.1
  11.9 0.0 all-gather.3.cloned.1.call-update
  11.9 0.0 copy-done.3
  11.9 14.5 %all_to_all.10.got = f32[16,72,128]{2,1,0:T(8,128)} all-to-all(f32[16,72,128]{2,1,0:T(8,128)S(1)} %copy-done.3), channel_id=1, replica_groups=mesh['front'=16,'row'=4,'col'=4] {'row','col'}, dimensions={0} | all-to-all | bytes 1179648 | tf_op jit(solution)/shard_map/all_to_all | solution.py:351
  26.4 6.8 %all-to-all-start.1 = ((f32[16,200,128]{2,1,0:T(8,128)}), f32[16,200,128]{2,1,0:T(8,128)S(1)}, u32[]{:S(2)}, u32[]{:S(2)}) async-start(f32[16,200,128]{2,1,0:T(8,128)} %get-tuple-element.27), calls=%async_computation.1 | async-start | bytes 3276800 | tf_op jit(solution)/shard_map/all_to_all | solution.py:359
  33.2 20.3 %shard_map.30 = (f32[512,512]{1,0:T(8,128)}, f32[512,512]{1,0:T(8,128)}) custom-call(f32[16,72,128]{2,1,0:T(8,128)} %all_to_all.10.got), custom_call_target="tpu_custom_call" | custom-call | tf_op jit(solution)/shard_map/pallas_call | solution.py:360
  53.5 3.6 %all-to-all-done.1.got = f32[16,200,128]{2,1,0:T(8,128)S(1)} async-done(((f32[16,200,128]{2,1,0:T(8,128)}), f32[16,200,128]{2,1,0:T(8,128)S(1)}, u32[]{:S(2)}, u32[]{:S(2)}) %all-to-all-start.1) | async-done | bytes 1638432 | tf_op jit(solution)/shard_map/all_to_all | solution.py:359
  57.1 0.0 copy-start
  57.1 0.0 copy-done.1
  57.1 0.0 collective-permute-start.2
  57.1 2.7 %collective-permute-start.1 = (f32[2,128,768]{2,1,0:T(8,128)S(1)}, f32[2,128,768]{2,1,0:T(8,128)}, u32[]{:S(2)}, u32[]{:S(2)}) collective-permute-start(f32[2,128,768]{2,1,0:T(8,128)S(1)} %copy-done.1), channel_id=1, source_target_pairs={{0,12},{4,0},{8,4},{12,8},{1,13},{5,1},{9,5},{13,9},{2,14},{6,2},{... | collective-permute-start | bytes 2359304 | tf_op jit(solution)/shard_map/ppermute | solution.py:362
  59.8 0.0 collective-permute-start
  59.8 0.0 copy-done
  59.8 22.8 %shard_map.31 = (f32[512,512]{1,0:T(8,128)}, f32[512,512]{1,0:T(8,128)}, f32[512,512]{1,0:T(8,128)}) custom-call(f32[16,200,128]{2,1,0:T(8,128)} %copy-done, f32[512,512]{1,0:T(8,128)} %get-tuple-element.32.inverse0.inv0), custom_call_target="tpu_custom_call" | custom-call | tf_op jit(solution)/shard_map/pallas_call | solution.py:363
  82.6 0.0 collective-permute-done.2.ac2
  82.6 0.0 copy-start.2
  82.6 10.9 %collective-permute-done.1.ac3 = f32[2,128,768]{2,1,0:T(8,128)} collective-permute-done((f32[2,128,768]{2,1,0:T(8,128)S(1)}, f32[2,128,768]{2,1,0:T(8,128)}, u32[]{:S(2)}, u32[]{:S(2)}) %collective-permute-start.1) | collective-permute-done | bytes 786464 | tf_op jit(solution)/shard_map/ppermute | solution.py:362
  93.5 1.5 %collective-permute-done.ac1 = f32[2,128,768]{2,1,0:T(8,128)} collective-permute-done((f32[2,128,768]{2,1,0:T(8,128)S(1)}, f32[2,128,768]{2,1,0:T(8,128)}, u32[]{:S(2)}, u32[]{:S(2)}) %collective-permute-start) | collective-permute-done | bytes 786464 | tf_op jit(solution)/shard_map/ppermute | solution.py:362
  95.0 0.0 copy-done.2
  95.0 18.9 %shard_map.32 = f32[8,128,8,128]{3,2,1,0:T(8,128)} custom-call(f32[8,128,8,128]{3,2,1,0:T(8,128)} %bitcast.7, s32[2,32,32]{2,1,0:T(8,128)} %pattern.1, f32[4,2,6,128,128]{4,3,2,1,0:T(8,128)} %bitcast.8, f32[2,128,768]{2,1,0:T(8,128)} %get-tuple-element.30.ac0, f32[2,128,768]{2,1,0:T(8,128)} %collective-permute-done.ac1, ...), custom_call_target="tpu_custom_call" | custom-call | tf_op jit(solution)/shard_map/pallas_call | solution.py:365
  (1 shorter events, 0.0 us)
Async XLA Ops:
  6.5 88.5 %all-gather.3.cloned.1.call-start = ((), (), s32[]{:S(2)}) async-start(), calls=%async_computation.2 | async-start | bytes 3932160 | tf_op jit(solution)/shard_map/all_gather | solution.py:357
  9.2 2.7 %copy-start.3 = (f32[16,72,128]{2,1,0:T(8,128)S(1)}, f32[16,72,128]{2,1,0:T(8,128)}, u32[]{:S(2)}) copy-start(f32[16,72,128]{2,1,0:T(8,128)} %get-tuple-element.26) | copy-start | bytes 1769476
  11.9 45.2 %copy-start.1 = (f32[2,128,768]{2,1,0:T(8,128)S(1)}, f32[2,128,768]{2,1,0:T(8,128)}, u32[]{:S(2)}) copy-start(f32[2,128,768]{2,1,0:T(8,128)} %get-tuple-element.30.ac0) | copy-start | bytes 2359300
  26.4 30.6 %all-to-all-start.1 = ((f32[16,200,128]{2,1,0:T(8,128)}), f32[16,200,128]{2,1,0:T(8,128)S(1)}, u32[]{:S(2)}, u32[]{:S(2)}) async-start(f32[16,200,128]{2,1,0:T(8,128)} %get-tuple-element.27), calls=%async_computation.1 | async-start | bytes 3276800 | tf_op jit(solution)/shard_map/all_to_all | solution.py:359
  57.1 2.7 %copy-start = (f32[16,200,128]{2,1,0:T(8,128)}, f32[16,200,128]{2,1,0:T(8,128)S(1)}, u32[]{:S(2)}) copy-start(f32[16,200,128]{2,1,0:T(8,128)S(1)} %all-to-all-done.1.got) | copy-start | bytes 4915204
  57.1 25.5 %collective-permute-start.2 = (f32[2,128,768]{2,1,0:T(8,128)S(1)}, f32[2,128,768]{2,1,0:T(8,128)S(1)}, u32[]{:S(2)}, u32[]{:S(2)}) collective-permute-start(f32[2,128,768]{2,1,0:T(8,128)S(1)} %copy-done.1), channel_id=1, source_target_pairs={{0,8},{4,12},{8,0},{12,4},{1,9},{5,13},{9,1},{13,5},{2,10},{6,14},... | collective-permute-start | bytes 2359304 | tf_op jit(solution)/shard_map/ppermute | solution.py:362
  57.1 36.4 %collective-permute-start.1 = (f32[2,128,768]{2,1,0:T(8,128)S(1)}, f32[2,128,768]{2,1,0:T(8,128)}, u32[]{:S(2)}, u32[]{:S(2)}) collective-permute-start(f32[2,128,768]{2,1,0:T(8,128)S(1)} %copy-done.1), channel_id=1, source_target_pairs={{0,12},{4,0},{8,4},{12,8},{1,13},{5,1},{9,5},{13,9},{2,14},{6,2},{... | collective-permute-start | bytes 2359304 | tf_op jit(solution)/shard_map/ppermute | solution.py:362
  59.8 35.2 %collective-permute-start = (f32[2,128,768]{2,1,0:T(8,128)S(1)}, f32[2,128,768]{2,1,0:T(8,128)}, u32[]{:S(2)}, u32[]{:S(2)}) collective-permute-start(f32[2,128,768]{2,1,0:T(8,128)S(1)} %copy-done.1), channel_id=1, source_target_pairs={{0,4},{4,8},{8,12},{12,0},{1,5},{5,9},{9,13},{13,1},{2,6},{6,10},{... | collective-permute-start | bytes 2359304 | tf_op jit(solution)/shard_map/ppermute | solution.py:362
  82.6 12.4 %copy-start.2 = (f32[2,128,768]{2,1,0:T(8,128)}, f32[2,128,768]{2,1,0:T(8,128)S(1)}, u32[]{:S(2)}) copy-start(f32[2,128,768]{2,1,0:T(8,128)S(1)} %collective-permute-done.2.ac2) | copy-start | bytes 2359300
Sparse Core Ops, SparseCore 0:
  12.0 59.1 all-gather.2
where the time goes:
time: 121 us
  Pallas kernels  67.2 us (56%)
  waiting for transfers between devices  16 us (13%)
  blocking collectives  14.5 us (12%)
  between operations  13.5 us (11%)
  starting transfers between devices  9.51 us (8%)
    pallas_call x1, Pallas kernels, per_device(): across, low1, inv1 = call(second_kernel, [square] * 3, work)(got1, inv0)  22.8 us
    pallas_call x1, Pallas kernels, per_device(): low0, inv0 = call(first_kernel, [square] * 2, work)(got0)  20.3 us
    pallas_call x1, Pallas kernels, per_device(): call(last_kernel, shape(LB, EDGE, LB, EDGE), [vmem(LB, EDGE, LB, EDGE), v...  18.9 us
    all_to_all x1, blocking collectives, per_device(): got0 = lax.all_to_all(c0, ('row', 'col'), 0, 0, tiled=True)  14.5 us
    ppermute x3, waiting for transfers between devices, per_device(): lax.ppermute(ac, 'row', [(i, (i + s) % GROUPS) for i in range(GROUPS)])  12.4 us
    all_to_all x1, starting transfers between devices, per_device(): got1 = lax.all_to_all(c1, ('row', 'col'), 0, 0, tiled=True)  6.78 us
    all_to_all x1, waiting for transfers between devices, per_device(): got1 = lax.all_to_all(c1, ('row', 'col'), 0, 0, tiled=True)  3.58 us
    ppermute x3, starting transfers between devices, per_device(): lax.ppermute(ac, 'row', [(i, (i + s) % GROUPS) for i in range(GROUPS)])  2.72 us
  transfers between devices with their start and end apart: 5, of which 3 were waited for; matrix products, arithmetic and copies ran while one was open for 0% of the time, Pallas kernels for 36%

commit v1 on v0

--- a/solution.py
+++ b/solution.py
@@ -55,14 +55,20 @@
 def factor_block(a, w):
     sub = lax.broadcasted_iota(jnp.int32, (TILE, EDGE), 0)
     count = EDGE // TILE
-    left, right = a[:TILE, :], w[:TILE, :]
+
+    def tile(p):
+        return slice(TILE * p, TILE * (p + 1))
+
+    def columns(x, p):
+        return [spread(x[:, TILE * p + q:TILE * p + q + 1]) for q in range(TILE)]
+
+    rows = [(a[tile(p), :], w[tile(p), :]) for p in range(2)]
+    cols = columns(rows[0][0], 0)
     for p in range(count):
-        at, after = slice(TILE * p, TILE * (p + 1)), slice(TILE * (p + 1), TILE * (p + 2))
-        more = p + 1 < count
-        cols = [spread(left[:, TILE * p + q:TILE * p + q + 1]) for q in range(TILE)]
-        if more:
-            next_left, next_right = a[after, :], w[after, :]
-            next_cols = [spread(next_left[:, TILE * p + q:TILE * p + q + 1]) for q in range(TILE)]
+        if p + 2 < count:
+            rows.append((a[tile(p + 2), :], w[tile(p + 2), :]))
+        below = [columns(left, p) for left, _ in rows[1:]]
+        corner = columns(rows[1][0], p + 1) if len(rows) > 1 else None
         invs = jnp.zeros((TILE, EDGE), F32)
         pivot = spread(cols[0][:1, :])
         for q in range(TILE):
@@ -70,22 +76,20 @@
             if q + 1 < TILE:
                 beside = spread(cols[q + 1][q:q + 1, :])
                 pivot = spread(cols[q + 1][q + 1:q + 2, :]) - (beside * beside) * inv
-            m = jnp.where(sub > q, cols[q], 0.0) * inv
             invs = jnp.where(sub == q, inv, invs)
-            row_left, row_right = spread(left[q:q + 1, :]), spread(right[q:q + 1, :])
-            left, right = left - m * row_left, right - m * row_right
-            if more:
-                n = next_cols[q] * inv
-                next_left, next_right = next_left - n * row_left, next_right - n * row_right
+            factors = [jnp.where(sub > q, cols[q], 0.0) * inv] + [one[q] * inv for one in below]
+            left, right = (spread(x[q:q + 1, :]) for x in rows[0])
+            rows = [(x - m * left, y - m * right) for (x, y), m in zip(rows, factors)]
+            if corner is not None:
+                corner = [x - factors[1] * spread(below[0][q][t:t + 1, :]) for t, x in enumerate(corner)]
             for t in range(q + 1, TILE):
                 across = spread(cols[t][q:q + 1, :])
-                cols[t] = cols[t] - m * across
-                if more:
-                    next_cols[t] = next_cols[t] - n * across
+                for one, m in zip([cols] + below, factors):
+                    one[t] = one[t] - m * across
         root = lax.rsqrt(invs) * invs
-        left, right = left * root, right * root
-        a[at, :], w[at, :] = left, right
-        low = TILE * (p + 2)
+        left, right = rows[0][0] * root, rows[0][1] * root
+        a[tile(p), :], w[tile(p), :] = left, right
+        low = TILE * (p + 3)
         if low < EDGE:
             h, m, l = split3(left)
             vh, vm, vl = split3(right)
@@ -95,17 +99,20 @@
             change = lax.dot_general(lhs, rhs, TN, preferred_element_type=F32)
             a[low:, :] = a[low:, :] - change[low:, :EDGE]
             w[low:, :] = w[low:, :] - change[low:, EDGE:]
-        if more:
-            left, right = next_left, next_right
-
-
-def factor_panel(s, lower, inverse, a, w):
+        rows, cols = rows[1:], corner
+
+
+def factor_panel(s, lower, inverse, a, w, low_out, inv_out, sem):
     ri = lax.broadcasted_iota(jnp.int32, (EDGE, EDGE), 0)
     ci = lax.broadcasted_iota(jnp.int32, (EDGE, EDGE), 1)
+    copies = []
     for k in range(GROUPS):
         here = slice(k * EDGE, (k + 1) * EDGE)
         below = slice((k + 1) * EDGE, WIDTH)
         before = slice(0, k * EDGE)
+        if k + 1 < GROUPS:
+            lower[here, below] = jnp.zeros((EDGE, WIDTH - (k + 1) * EDGE), F32)
+            inverse[here, below] = jnp.zeros((EDGE, WIDTH - (k + 1) * EDGE), F32)
         a[k] = s[here, here]
         w[k] = jnp.where(ri == ci, 1.0, 0.0)
         factor_block(a.at[k], w.at[k])
@@ -114,13 +121,16 @@
             part = exact_dot(s[below, here], d, NT)
             lower[below, here] = part
             s[below, below] = s[below, below] - exact_dot(part, part, NT)
-            lower[here, below] = jnp.zeros((EDGE, WIDTH - (k + 1) * EDGE), F32)
-            inverse[here, below] = jnp.zeros((EDGE, WIDTH - (k + 1) * EDGE), F32)
         lower[here, here] = jnp.where(ri <= ci, a[k], 0.0).T
         inverse[here, here] = d
         if k > 0:
             part = exact_dot(lower[here, before], inverse[before, before], NN)
             inverse[here, before] = -exact_dot(d, part, NN)
+        for i, (held, to) in enumerate(((lower, low_out), (inverse, inv_out))):
+            copies.append(pltpu.make_async_copy(held.at[here], to.at[here], sem.at[2 * k + i]))
+            copies[-1].start()
+    for copy in copies:
+        copy.wait()
 
 
 def pack(block, ref, r, c):
@@ -142,30 +152,41 @@
     return jnp.where((row == lane) & (row < HALF), jnp.broadcast_to(got[HALF:HALF + 1], (EDGE, EDGE)), whole)
 
 
-def unpack(got, at, s):
+def unpack(got, s):
     for r in range(GROUPS):
         for c in range(r):
             span = slice(c * EDGE, (c + 1) * EDGE)
-            s[r * EDGE:r * EDGE + HALF, span] = got[r * GROUPS + c, at:at + HALF]
-            s[r * EDGE + HALF:(r + 1) * EDGE, span] = got[c * GROUPS + r, at:at + HALF]
+            s[r * EDGE:r * EDGE + HALF, span] = got[r * GROUPS + c, 0:HALF]
+            s[r * EDGE + HALF:(r + 1) * EDGE, span] = got[c * GROUPS + r, 0:HALF]
         span = slice(r * EDGE, (r + 1) * EDGE)
-        s[span, span] = unpack_diagonal(got[r * GROUPS + r, at:at + HELD])
-
-
-def first_kernel(got, lower, inverse, s, a, w):
-    unpack(got, 0, s)
-    factor_panel(s, lower, inverse, a, w)
-
-
-def second_kernel(got, inverse0, across, lower, inverse, s, a, w):
+        s[span, span] = unpack_diagonal(got[r * GROUPS + r, 0:HELD])
+
+
+def first_kernel(got, low_out, inv_out, s, lower, inverse, a, w, sem):
+    unpack(got, s)
+    factor_panel(s, lower, inverse, a, w, low_out, inv_out, sem)
+
+
+def second_kernel(got, inverse0, across_out, low_out, inv_out, s, lower, inverse, a, w, sem, rect, square, across, invs, sem2):
+    loads = [pltpu.make_async_copy(*pair, sem2.at[i]) for i, pair in enumerate(
+        ((inverse0, invs), (got.at[:, :EDGE], rect), (got.at[:, EDGE:], square)))]
+    for load in loads:
+        load.start()
+    loads[0].wait()
+    inv = split2(invs[...])
+    loads[1].wait()
     for r in range(GROUPS):
         for c in range(GROUPS):
-            s[r * EDGE:(r + 1) * EDGE, c * EDGE:(c + 1) * EDGE] = got[r * GROUPS + c, :EDGE]
-    across[...] = dot3(split2(s[...]), split2(inverse0[...]), NT)
-    unpack(got, EDGE, s)
+            s[r * EDGE:(r + 1) * EDGE, c * EDGE:(c + 1) * EDGE] = rect[r * GROUPS + c]
+    across[...] = dot3(split2(s[...]), inv, NT)
+    store = pltpu.make_async_copy(across, across_out, sem2.at[3])
+    store.start()
+    loads[2].wait()
+    unpack(square, s)
     part = split2(across[...])
     s[...] = s[...] - dot3(part, part, NT)
-    factor_panel(s, lower, inverse, a, w)
+    factor_panel(s, lower, inverse, a, w, low_out, inv_out, sem)
+    store.wait()
 
 
 def collect(ids, at, flags):
@@ -212,8 +233,8 @@
     buf[0, :, 0, :] = low0[mine, own]
     buf[1, :, 0, :] = across[mine, own]
     buf[1, :, 1, :] = low1[mine, own]
-    stores = [pltpu.make_async_copy(buf.at[:NPAN], out.at[:NPAN], leave.at[0])]
-    stores[0].start()
+    store = pltpu.make_async_copy(buf.at[:NPAN], out.at[:NPAN], leave.at[0])
+    store.start()
     bh[...], bl[...] = split2(across[...])
     side = [(l, g) for l in range(REST) for g in range(GROUPS)]
     row_end = collect(ids, 0, [
@@ -275,10 +296,10 @@
         for l in range(REST):
             buf[l + NPAN, :, k, :] = lr[l * EDGE:(l + 1) * EDGE, own]
     visit(ids, col_end, all_end, product, target)
-    stores.append(pltpu.make_async_copy(buf.at[NPAN:], out.at[NPAN:], leave.at[1]))
-    stores[-1].start()
-    for store in stores:
-        store.wait()
+    last = pltpu.make_async_copy(buf.at[NPAN:], out.at[NPAN:], leave.at[1])
+    last.start()
+    store.wait()
+    last.wait()
 
 
 def run(copies):
@@ -338,10 +359,10 @@
 
 def per_device(front, pattern):
     blocks = front[0, :, :, 0]
-    work = [vmem(WIDTH, WIDTH), vmem(GROUPS, EDGE, EDGE), vmem(GROUPS, EDGE, EDGE)]
     square = shape(WIDTH, WIDTH)
     every = GROUPS * GROUPS
     away, dma = pl.BlockSpec(memory_space=pltpu.HBM), pltpu.SemaphoreType.DMA
+    work = [vmem(WIDTH, WIDTH)] * 3 + [vmem(GROUPS, EDGE, EDGE)] * 2 + [dma((LB,))]
     c0, c1 = call(
         corner_kernel, [shape(every, HELD, EDGE), shape(every, EDGE + HELD, EDGE)],
         [vmem(EDGE, EDGE), vmem(HELD, EDGE), vmem(EDGE, EDGE), vmem(HELD, EDGE), vmem(EDGE + HELD, EDGE), dma((3 + 2 * every,))],
@@ -355,12 +376,17 @@
         in_specs=[away], out_specs=[away, away],
     )(later)
     ar = lax.all_gather(ar, "col", axis=0)
-    c1, got0 = lax.optimization_barrier((c1, got0))
+    c1, ac, got0 = lax.optimization_barrier((c1, ac, got0))
     got1 = lax.all_to_all(c1, ("row", "col"), 0, 0, tiled=True)
-    low0, inv0 = call(first_kernel, [square] * 2, work)(got0)
-    ac, got1, inv0 = lax.optimization_barrier((ac, got1, inv0))
-    acs = [ac] + [lax.ppermute(ac, "row", [(i, (i + s) % GROUPS) for i in range(GROUPS)]) for s in (1, 3, 2)]
-    across, low1, inv1 = call(second_kernel, [square] * 3, work)(got1, inv0)
+    low0, inv0 = call(first_kernel, [square] * 2, work, out_specs=[away] * 2)(got0)
+    later, inv0 = lax.optimization_barrier((ac, inv0))
+    acs = [ac] + [lax.ppermute(piece, "row", [(i, (i + s) % GROUPS) for i in range(GROUPS)])
+                  for s, piece in ((1, later), (3, later), (2, ac))]
+    across, low1, inv1 = call(
+        second_kernel, [square] * 3,
+        work + [vmem(every, EDGE, EDGE), vmem(every, HELD, EDGE), vmem(WIDTH, WIDTH), vmem(WIDTH, WIDTH), dma((4,))],
+        in_specs=[away] * 2, out_specs=[away] * 3,
+    )(got1, inv0)
     whole = pl.BlockSpec(memory_space=pltpu.VMEM)
     result = call(
         last_kernel, shape(LB, EDGE, LB, EDGE),

time: 121 us -> 114 us (0.942)
  the two profiles are of different devices: /device:TPU:213 before, /device:TPU:112 now
where the time goes in v1:
time: 114 us; the launch traced here: 113 us
  Pallas kernels  56.5 us (50%)
  blocking collectives  17.6 us (15%)
  between operations  13.5 us (12%)
  waiting for transfers between devices  12.9 us (11%)
  starting transfers between devices  10.9 us (10%)
  local copies, waits for them, and re-layouts  2 us (2%)
    pallas_call x1, Pallas kernels, per_device(): call(second_kernel, [square] * 3, work + [vmem(every, EDGE, EDGE), vmem(e...  19.4 us
    all_to_all x1, blocking collectives, per_device(): got0 = lax.all_to_all(c0, ('row', 'col'), 0, 0, tiled=True)  17.6 us
    pallas_call x1, Pallas kernels, per_device(): call(first_kernel, [square] * 2, work, out_specs=[away] * 2)(got0)  16.8 us
    pallas_call x1, Pallas kernels, per_device(): call(last_kernel, shape(LB, EDGE, LB, EDGE), [vmem(LB, EDGE, LB, EDGE), v...  15 us
    all_to_all x1, waiting for transfers between devices, per_device(): got1 = lax.all_to_all(c1, ('row', 'col'), 0, 0, tiled=True)  12.8 us
    all_to_all x1, starting transfers between devices, per_device(): got1 = lax.all_to_all(c1, ('row', 'col'), 0, 0, tiled=True)  5.55 us
    ppermute x3, starting transfers between devices, per_device(): lax.ppermute(piece, 'row', [(i, (i + s) % GROUPS) for i in range(GROUPS)])  5.39 us
    pallas_call x1, Pallas kernels, per_device(): call(extract_kernel, [shape(NPAN, REST, EDGE, EDGE), shape(NPAN, EDGE, RO...  2.68 us
  transfers between devices with their start and end apart: 5, of which 1 were waited for; matrix products, arithmetic and copies ran while one was open for 0% of the time, Pallas kernels for 32%

profile of v1, /device:TPU:112, one launch (start us, length us, event | category | flops | bytes accessed | tf_op | source)
XLA Modules:
  0.0 113.4 jit_solution(16367371107813754815)
XLA Ops:
  6.5 0.0 all-gather.3.cloned.1.call-start
  6.5 2.6 %shard_map.28 = (f32[16,72,128]{2,1,0:T(8,128)}, f32[16,200,128]{2,1,0:T(8,128)}) custom-call(f32[8,128,8,128]{3,2,1,0:T(8,128)} %bitcast.5), custom_call_target="tpu_custom_call" | custom-call | tf_op jit(solution)/shard_map/pallas_call | solution.py:366
  9.2 0.0 copy-start.3
  9.2 2.7 %shard_map.29 = (f32[2,6,128,128]{3,2,1,0:T(8,128)}, f32[2,128,768]{2,1,0:T(8,128)}) custom-call(f32[8,128,8,128]{3,2,1,0:T(8,128)} %bitcast.6), custom_call_target="tpu_custom_call" | custom-call | tf_op jit(solution)/shard_map/pallas_call | solution.py:373
  11.9 0.0 copy-start.1
  11.9 0.0 all-gather.3.cloned.1.call-update
  11.9 0.0 copy-done.3
  11.9 17.6 %all_to_all.10.got = f32[16,72,128]{2,1,0:T(8,128)} all-to-all(f32[16,72,128]{2,1,0:T(8,128)S(1)} %copy-done.3), channel_id=1, replica_groups=mesh['front'=16,'row'=4,'col'=4] {'row','col'}, dimensions={0} | all-to-all | bytes 1179648 | tf_op jit(solution)/shard_map/all_to_all | solution.py:372
  29.5 5.6 %all-to-all-start.1 = ((f32[16,200,128]{2,1,0:T(8,128)}), f32[16,200,128]{2,1,0:T(8,128)S(1)}, u32[]{:S(2)}, u32[]{:S(2)}) async-start(f32[16,200,128]{2,1,0:T(8,128)} %get-tuple-element.33), calls=%async_computation.1 | async-start | bytes 3276800 | tf_op jit(solution)/shard_map/all_to_all | solution.py:380
  35.0 0.0 copy-done.1
  35.0 3.1 %collective-permute-start.2 = (f32[2,128,768]{2,1,0:T(8,128)S(1)}, f32[2,128,768]{2,1,0:T(8,128)S(1)}, u32[]{:S(2)}, u32[]{:S(2)}) collective-permute-start(f32[2,128,768]{2,1,0:T(8,128)S(1)} %copy-done.1), channel_id=1, source_target_pairs={{0,8},{4,12},{8,0},{12,4},{1,9},{5,13},{9,1},{13,5},{2,10},{6,14},... | collective-permute-start | bytes 2359304 | tf_op jit(solution)/shard_map/ppermute | solution.py:383
  38.2 16.8 %shard_map.30 = (f32[512,512]{1,0:T(8,128)}, f32[512,512]{1,0:T(8,128)}) custom-call(f32[16,72,128]{2,1,0:T(8,128)} %all_to_all.10.got), custom_call_target="tpu_custom_call" | custom-call | tf_op jit(solution)/shard_map/pallas_call | solution.py:381
  55.0 1.4 %collective-permute-start.1 = (f32[2,128,768]{2,1,0:T(8,128)S(1)}, f32[2,128,768]{2,1,0:T(8,128)}, u32[]{:S(2)}, u32[]{:S(2)}) collective-permute-start(f32[2,128,768]{2,1,0:T(8,128)S(1)} %copy-done.1), channel_id=1, source_target_pairs={{0,12},{4,0},{8,4},{12,8},{1,13},{5,1},{9,5},{13,9},{2,14},{6,2},{... | collective-permute-start | bytes 2359304 | tf_op jit(solution)/shard_map/ppermute | solution.py:383
  56.4 0.9 collective-permute-start
  57.3 12.8 %all-to-all-done.1.got = f32[16,200,128]{2,1,0:T(8,128)S(1)} async-done(((f32[16,200,128]{2,1,0:T(8,128)}), f32[16,200,128]{2,1,0:T(8,128)S(1)}, u32[]{:S(2)}, u32[]{:S(2)}) %all-to-all-start.1) | async-done | bytes 1638432 | tf_op jit(solution)/shard_map/all_to_all | solution.py:380
  70.1 1.2 %copy-done = f32[16,200,128]{2,1,0:T(8,128)} copy-done((f32[16,200,128]{2,1,0:T(8,128)}, f32[16,200,128]{2,1,0:T(8,128)S(1)}, u32[]{:S(2)}) %copy-start) | copy-done | bytes 1638424
  71.3 19.4 %shard_map.31 = (f32[512,512]{1,0:T(8,128)}, f32[512,512]{1,0:T(8,128)}, f32[512,512]{1,0:T(8,128)}) custom-call(f32[16,200,128]{2,1,0:T(8,128)} %copy-done, f32[512,512]{1,0:T(8,128)} %get-tuple-element.32.inverse0.inv0), custom_call_target="tpu_custom_call" | custom-call | tf_op jit(solution)/shard_map/pallas_call | solution.py:385
  90.7 0.0 collective-permute-done.2.ac2
  90.7 0.0 copy-start.2
  90.7 0.0 collective-permute-done.1.ac3
  90.7 0.0 collective-permute-done.ac1
  90.7 0.0 all-gather.3.cloned.1.call-done
  90.7 0.8 copy-done.2
  91.6 15.0 %shard_map.32 = f32[8,128,8,128]{3,2,1,0:T(8,128)} custom-call(f32[8,128,8,128]{3,2,1,0:T(8,128)} %bitcast.7, s32[2,32,32]{2,1,0:T(8,128)} %pattern.1, f32[4,2,6,128,128]{4,3,2,1,0:T(8,128)} %bitcast.8, f32[2,128,768]{2,1,0:T(8,128)} %get-tuple-element.30.ac0, f32[2,128,768]{2,1,0:T(8,128)} %collective-permute-done.ac1, ...), custom_call_target="tpu_custom_call" | custom-call | tf_op jit(solution)/shard_map/pallas_call | solution.py:391
  (1 shorter events, 0.0 us)
Async XLA Ops:
  6.5 84.2 %all-gather.3.cloned.1.call-start = ((), (), s32[]{:S(2)}) async-start(), calls=%async_computation.2 | async-start | bytes 3932160 | tf_op jit(solution)/shard_map/all_gather | solution.py:378
  9.2 2.7 %copy-start.3 = (f32[16,72,128]{2,1,0:T(8,128)S(1)}, f32[16,72,128]{2,1,0:T(8,128)}, u32[]{:S(2)}) copy-start(f32[16,72,128]{2,1,0:T(8,128)} %get-tuple-element.26) | copy-start | bytes 1769476
  11.9 23.2 %copy-start.1 = (f32[2,128,768]{2,1,0:T(8,128)S(1)}, f32[2,128,768]{2,1,0:T(8,128)}, u32[]{:S(2)}) copy-start(f32[2,128,768]{2,1,0:T(8,128)} %get-tuple-element.30.ac0) | copy-start | bytes 2359300
  29.5 40.6 %all-to-all-start.1 = ((f32[16,200,128]{2,1,0:T(8,128)}), f32[16,200,128]{2,1,0:T(8,128)S(1)}, u32[]{:S(2)}, u32[]{:S(2)}) async-start(f32[16,200,128]{2,1,0:T(8,128)} %get-tuple-element.33), calls=%async_computation.1 | async-start | bytes 3276800 | tf_op jit(solution)/shard_map/all_to_all | solution.py:380
  35.0 55.6 %collective-permute-start.2 = (f32[2,128,768]{2,1,0:T(8,128)S(1)}, f32[2,128,768]{2,1,0:T(8,128)S(1)}, u32[]{:S(2)}, u32[]{:S(2)}) collective-permute-start(f32[2,128,768]{2,1,0:T(8,128)S(1)} %copy-done.1), channel_id=1, source_target_pairs={{0,8},{4,12},{8,0},{12,4},{1,9},{5,13},{9,1},{13,5},{2,10},{6,14},... | collective-permute-start | bytes 2359304 | tf_op jit(solution)/shard_map/ppermute | solution.py:383
  55.0 35.7 %collective-permute-start.1 = (f32[2,128,768]{2,1,0:T(8,128)S(1)}, f32[2,128,768]{2,1,0:T(8,128)}, u32[]{:S(2)}, u32[]{:S(2)}) collective-permute-start(f32[2,128,768]{2,1,0:T(8,128)S(1)} %copy-done.1), channel_id=1, source_target_pairs={{0,12},{4,0},{8,4},{12,8},{1,13},{5,1},{9,5},{13,9},{2,14},{6,2},{... | collective-permute-start | bytes 2359304 | tf_op jit(solution)/shard_map/ppermute | solution.py:383
  56.4 34.3 %collective-permute-start = (f32[2,128,768]{2,1,0:T(8,128)S(1)}, f32[2,128,768]{2,1,0:T(8,128)}, u32[]{:S(2)}, u32[]{:S(2)}) collective-permute-start(f32[2,128,768]{2,1,0:T(8,128)S(1)} %copy-done.1), channel_id=1, source_target_pairs={{0,4},{4,8},{8,12},{12,0},{1,5},{5,9},{9,13},{13,1},{2,6},{6,10},{... | collective-permute-start | bytes 2359304 | tf_op jit(solution)/shard_map/ppermute | solution.py:383
  70.1 1.2 %copy-start = (f32[16,200,128]{2,1,0:T(8,128)}, f32[16,200,128]{2,1,0:T(8,128)S(1)}, u32[]{:S(2)}) copy-start(f32[16,200,128]{2,1,0:T(8,128)S(1)} %all-to-all-done.1.got) | copy-start | bytes 4915204
  90.7 0.9 copy-start.2
Sparse Core Ops, SparseCore 0:
  12.0 60.3 all-gather.2

commit v2 on v1

--- a/solution.py
+++ b/solution.py
@@ -212,18 +212,64 @@
     return pl.ds(pl.multiple_of(i * EDGE, EDGE), EDGE)
 
 
-def last_kernel(front, pattern, ar, ac0, ac1, ac3, ac2, low0, inv0, across, low1, inv1, out,
-                buf, arv, acv, xh, xl, yh, yl, th, tl, sh, sl, bh, bl, lr, lc, ids, arrive, leave):
+def unpair(number):
+    return lax.div(number, TILE), lax.rem(number, TILE)
+
+
+SIDE = [(l, g) for l in range(REST) for g in range(GROUPS)]
+
+
+def row_kernel(ar, pattern, inv0, across, inv1, xh_out, xl_out, mine_out,
+               arv, xh, xl, th, tl, bh, bl, lr, mine, ids, arrive, leave):
+    r, own = lax.axis_index("row"), spans(lax.axis_index("col"))
+    half = WIDTH // 2
+    loads = [pltpu.make_async_copy(ar.at[:, k], arv.at[:, k], arrive.at[k]) for k in range(NPAN)]
+    for load in loads:
+        load.start()
+    bh[...], bl[...] = split2(across[...])
+    end = collect(ids, 0, [(l * TILE + g, pattern[0, (l + NPAN) * GROUPS + r, GROUPS + g] > 0) for l, g in SIDE])
+
+    def product(number):
+        l, g = unpair(number)
+        return dot3((xh[0, spans(l), :], xl[0, spans(l), :]), (bh[spans(g), :], bl[spans(g), :]), NT)
+
+    def target(number, change):
+        l, g = unpair(number)
+        arv[g, 1, l] = arv[g, 1, l] - change
+
+    stores = []
+    for k in range(NPAN):
+        loads[k].wait()
+        if k == 1:
+            visit(ids, 0, end, product, target)
+        for g in range(GROUPS):
+            span = slice(g * EDGE, (g + 1) * EDGE)
+            th[:, span], tl[:, span] = split2(arv[g, k].reshape(ROWS, EDGE))
+        wh, wl = split2((inv0, inv1)[k][...])
+        lr[:, :half] = dot3((th[:, :half], tl[:, :half]), (wh[:half, :half], wl[:half, :half]), NT)
+        lr[:, half:] = dot3((th[...], tl[...]), (wh[half:, :], wl[half:, :]), NT)
+        xh[k], xl[k] = split2(lr[...])
+        mine[k] = lr[:, own]
+        for i, (held, to) in enumerate(((xh, xh_out), (xl, xl_out), (mine, mine_out))):
+            stores.append(pltpu.make_async_copy(held.at[k], to.at[k], leave.at[3 * k + i]))
+            stores[-1].start()
+    for store in stores:
+        store.wait()
+
+
+def last_kernel(front, pattern, xh_in, xl_in, own_cols, ac0, ac1, ac3, ac2, low0, inv0, across, low1, inv1, out,
+                buf, acv, xh, xl, yh, yl, sh, sl, bh, bl, held, lc, ids, arrive, leave):
     r, c = lax.axis_index("row"), lax.axis_index("col")
     own, mine = spans(c), spans(r)
     half = WIDTH // 2
     loads = []
     for k in range(NPAN):
-        loads.append(pltpu.make_async_copy(ar.at[:, k], arv.at[:, k], arrive.at[8 * k]))
-        for s, ac in ((0, ac0), (1, ac1), (2, ac2), (3, ac3)):
-            loads.append(pltpu.make_async_copy(ac.at[k], acv.at[(r + GROUPS - s) % GROUPS, k], arrive.at[8 * k + s + 1]))
+        loads.append([pltpu.make_async_copy(ac.at[k], acv.at[(r + GROUPS - s) % GROUPS, k], arrive.at[4 * k + s])
+                      for s, ac in ((0, ac0), (1, ac1), (2, ac2), (3, ac3))])
+    copies = [pltpu.make_async_copy(*pair, arrive.at[8 + i])
+              for i, pair in enumerate(((own_cols, held), (xh_in, xh), (xl_in, xl)))]
     fronts = [pltpu.make_async_copy(front.at[l], buf.at[l], arrive.at[16 + l]) for l in range(NPAN, LB)]
-    for load in loads + fronts:
+    for load in loads[0] + loads[1] + copies + fronts:
         load.start()
     zero = jnp.zeros((EDGE, EDGE), F32)
     for l in range(NPAN):
@@ -236,34 +282,22 @@
     store = pltpu.make_async_copy(buf.at[:NPAN], out.at[:NPAN], leave.at[0])
     store.start()
     bh[...], bl[...] = split2(across[...])
-    side = [(l, g) for l in range(REST) for g in range(GROUPS)]
-    row_end = collect(ids, 0, [
-        (l * TILE + g, pattern[0, (l + NPAN) * GROUPS + r, GROUPS + g] > 0) for l, g in side])
-    col_end = collect(ids, row_end, [
-        (l * TILE + g, pattern[0, GROUPS + g, (l + NPAN) * GROUPS + c] > 0) for l, g in side])
+    col_end = collect(ids, 0, [(l * TILE + g, pattern[0, GROUPS + g, (l + NPAN) * GROUPS + c] > 0) for l, g in SIDE])
     all_end = collect(ids, col_end, [
         ((k * TILE + l) * TILE + m, pattern[k, (l + NPAN) * GROUPS + r, (m + NPAN) * GROUPS + c] > 0)
         for k in range(NPAN) for l in range(REST) for m in range(REST)])
 
-    def row_product(number):
-        l, g = lax.div(number, TILE), lax.rem(number, TILE)
-        return dot3((xh[0, spans(l), :], xl[0, spans(l), :]), (bh[spans(g), :], bl[spans(g), :]), NT)
-
-    def row_target(number, change):
-        l, g = lax.div(number, TILE), lax.rem(number, TILE)
-        arv[g, 1, l] = arv[g, 1, l] - change
-
     def col_product(number):
-        l, g = lax.div(number, TILE), lax.rem(number, TILE)
+        l, g = unpair(number)
         return dot3((bh[spans(g), :], bl[spans(g), :]), (yh[0, :, spans(l)], yl[0, :, spans(l)]), NN)
 
     def col_target(number, change):
-        l, g = lax.div(number, TILE), lax.rem(number, TILE)
+        l, g = unpair(number)
         acv[g, 1, :, spans(l)] = acv[g, 1, :, spans(l)] - change
 
     def place(number):
-        row = lax.div(number, TILE)
-        return lax.div(row, TILE), lax.rem(row, TILE), lax.rem(number, TILE)
+        row, m = unpair(number)
+        return unpair(row) + (m,)
 
     def product(number):
         k, l, m = place(number)
@@ -274,27 +308,22 @@
         buf[l + NPAN, :, m + NPAN, :] = buf[l + NPAN, :, m + NPAN, :] - change
 
     for k in range(NPAN):
-        for load in loads[5 * k:5 * k + 5]:
+        for load in loads[k]:
             load.wait()
         if k == 1:
-            visit(ids, 0, row_end, row_product, row_target)
-            visit(ids, row_end, col_end, col_product, col_target)
+            visit(ids, 0, col_end, col_product, col_target)
         for g in range(GROUPS):
             span = slice(g * EDGE, (g + 1) * EDGE)
-            th[:, span], tl[:, span] = split2(arv[g, k].reshape(ROWS, EDGE))
             sh[span, :], sl[span, :] = split2(acv[g, k])
         wh, wl = split2((inv0, inv1)[k][...])
-        lr[:, :half] = dot3((th[:, :half], tl[:, :half]), (wh[:half, :half], wl[:half, :half]), NT)
-        lr[:, half:] = dot3((th[...], tl[...]), (wh[half:, :], wl[half:, :]), NT)
-        xh[k], xl[k] = split2(lr[...])
         lc[:half, :] = dot3((wh[:half, :half], wl[:half, :half]), (sh[:half, :], sl[:half, :]), NN)
         lc[half:, :] = dot3((wh[half:, :], wl[half:, :]), (sh[...], sl[...]), NN)
         yh[k], yl[k] = split2(lc[...])
-        if k == 0:
-            for load in fronts:
-                load.wait()
+    for load in copies + fronts:
+        load.wait()
+    for k in range(NPAN):
         for l in range(REST):
-            buf[l + NPAN, :, k, :] = lr[l * EDGE:(l + 1) * EDGE, own]
+            buf[l + NPAN, :, k, :] = held[k, l * EDGE:(l + 1) * EDGE, :]
     visit(ids, col_end, all_end, product, target)
     last = pltpu.make_async_copy(buf.at[NPAN:], out.at[NPAN:], leave.at[1])
     last.start()
@@ -387,16 +416,22 @@
         work + [vmem(every, EDGE, EDGE), vmem(every, HELD, EDGE), vmem(WIDTH, WIDTH), vmem(WIDTH, WIDTH), dma((4,))],
         in_specs=[away] * 2, out_specs=[away] * 3,
     )(got1, inv0)
-    whole = pl.BlockSpec(memory_space=pltpu.VMEM)
+    whole, scalars = pl.BlockSpec(memory_space=pltpu.VMEM), pl.BlockSpec(memory_space=pltpu.SMEM)
+    tall, flat, bound = [(NPAN, ROWS, WIDTH)] * 2, [(NPAN, WIDTH, ROWS)] * 2, [vmem(WIDTH, WIDTH, dtype=BF16)] * 2
+    xh, xl, own_cols = call(
+        row_kernel, [jax.ShapeDtypeStruct(dims, BF16) for dims in tall] + [shape(NPAN, ROWS, EDGE)],
+        [vmem(GROUPS, NPAN, REST, EDGE, EDGE)] + [vmem(*dims, dtype=BF16) for dims in tall]
+        + [vmem(ROWS, WIDTH, dtype=BF16)] * 2 + bound
+        + [vmem(ROWS, WIDTH), vmem(NPAN, ROWS, EDGE), pltpu.SMEM((32,), jnp.int32), dma((NPAN,)), dma((3 * NPAN,))],
+        in_specs=[away, scalars] + [whole] * 3, out_specs=[away] * 3,
+    )(ar, pattern, inv0, across, inv1)
     result = call(
         last_kernel, shape(LB, EDGE, LB, EDGE),
-        [vmem(LB, EDGE, LB, EDGE), vmem(GROUPS, NPAN, REST, EDGE, EDGE), vmem(GROUPS, NPAN, EDGE, ROWS)]
-        + [vmem(NPAN, ROWS, WIDTH, dtype=BF16)] * 2 + [vmem(NPAN, WIDTH, ROWS, dtype=BF16)] * 2 + [vmem(ROWS, WIDTH, dtype=BF16)] * 2
-        + [vmem(WIDTH, ROWS, dtype=BF16)] * 2 + [vmem(WIDTH, WIDTH, dtype=BF16)] * 2
-        + [vmem(ROWS, WIDTH), vmem(WIDTH, ROWS), pltpu.SMEM((128,), jnp.int32), dma((24,)), dma((2,))],
-        in_specs=[away, pl.BlockSpec(memory_space=pltpu.SMEM), away, away, away, away, away] + [whole] * 5,
-        out_specs=away,
-    )(blocks, pattern, ar, *acs, low0, inv0, across, low1, inv1)
+        [vmem(LB, EDGE, LB, EDGE), vmem(GROUPS, NPAN, EDGE, ROWS)] + [vmem(*dims, dtype=BF16) for dims in tall + flat]
+        + [vmem(WIDTH, ROWS, dtype=BF16)] * 2 + bound
+        + [vmem(NPAN, ROWS, EDGE), vmem(WIDTH, ROWS), pltpu.SMEM((128,), jnp.int32), dma((24,)), dma((2,))],
+        in_specs=[away, scalars] + [away] * 7 + [whole] * 5, out_specs=away,
+    )(blocks, pattern, xh, xl, own_cols, *acs, low0, inv0, across, low1, inv1)
     return result[None, :, :, None]
 
 

time: 114 us -> 119 us (1.044)
  Pallas kernels: 56.5 us -> 60.5 us
    pallas_call x0 -> x1, Pallas kernels: none -> 7.77 us  [per_device(): call(row_kernel, [jax.ShapeDtypeStruct(dims, BF16) for dims in tall] + [s...]
    pallas_call x1, Pallas kernels: 15 us -> 11.3 us  [per_device(): call(last_kernel, shape(LB, EDGE, LB, EDGE), [vmem(LB, EDGE, LB, EDGE), v...]
  transfers between devices with their start and end apart: 5 -> 5, of which waited for: 1 -> 1; matrix products, arithmetic and copies ran while one was open for 0% -> 0% of each run, Pallas kernels for 32% -> 37%
where the time goes in v2:
time: 119 us; the launch traced here: 117 us
  Pallas kernels  60.5 us (51%)
  blocking collectives  17.4 us (15%)
  between operations  13.5 us (11%)
  waiting for transfers between devices  12.9 us (11%)
  starting transfers between devices  11.2 us (9%)
  local copies, waits for them, and re-layouts  2.05 us (2%)
    pallas_call x1, Pallas kernels, per_device(): call(second_kernel, [square] * 3, work + [vmem(every, EDGE, EDGE), vmem(e...  19.3 us
    all_to_all x1, blocking collectives, per_device(): got0 = lax.all_to_all(c0, ('row', 'col'), 0, 0, tiled=True)  17.4 us
    pallas_call x1, Pallas kernels, per_device(): call(first_kernel, [square] * 2, work, out_specs=[away] * 2)(got0)  16.9 us
    all_to_all x1, waiting for transfers between devices, per_device(): got1 = lax.all_to_all(c1, ('row', 'col'), 0, 0, tiled=True)  12.8 us
    pallas_call x1, Pallas kernels, per_device(): call(last_kernel, shape(LB, EDGE, LB, EDGE), [vmem(LB, EDGE, LB, EDGE), v...  11.3 us
    pallas_call x1, Pallas kernels, per_device(): call(row_kernel, [jax.ShapeDtypeStruct(dims, BF16) for dims in tall] + [s...  7.77 us
    all_to_all x1, starting transfers between devices, per_device(): got1 = lax.all_to_all(c1, ('row', 'col'), 0, 0, tiled=True)  5.78 us
    ppermute x3, starting transfers between devices, per_device(): lax.ppermute(piece, 'row', [(i, (i + s) % GROUPS) for i in range(GROUPS)])  5.39 us
  transfers between devices with their start and end apart: 5, of which 1 were waited for; matrix products, arithmetic and copies ran while one was open for 0% of the time, Pallas kernels for 37%

profile of v2, /device:TPU:112, one launch (start us, length us, event | category | flops | bytes accessed | tf_op | source)
XLA Modules:
  0.0 117.5 jit_solution(17894417861969191901)
XLA Ops:
  6.5 0.0 all-gather.3.cloned.1.call-start
  6.5 2.6 %shard_map.28 = (f32[16,72,128]{2,1,0:T(8,128)}, f32[16,200,128]{2,1,0:T(8,128)}) custom-call(f32[8,128,8,128]{3,2,1,0:T(8,128)} %bitcast.5), custom_call_target="tpu_custom_call" | custom-call | tf_op jit(solution)/shard_map/pallas_call | solution.py:395
  9.2 0.0 copy-start.3
  9.2 2.6 %shard_map.29 = (f32[2,6,128,128]{3,2,1,0:T(8,128)}, f32[2,128,768]{2,1,0:T(8,128)}) custom-call(f32[8,128,8,128]{3,2,1,0:T(8,128)} %bitcast.6), custom_call_target="tpu_custom_call" | custom-call | tf_op jit(solution)/shard_map/pallas_call | solution.py:402
  11.8 0.0 all-gather.3.cloned.1.call-update
  11.8 0.0 copy-done.3
  11.8 17.4 %all_to_all.10.got = f32[16,72,128]{2,1,0:T(8,128)} all-to-all(f32[16,72,128]{2,1,0:T(8,128)S(1)} %copy-done.3), channel_id=1, replica_groups=mesh['front'=16,'row'=4,'col'=4] {'row','col'}, dimensions={0} | all-to-all | bytes 1179648 | tf_op jit(solution)/shard_map/all_to_all | solution.py:401
  29.2 5.8 %all-to-all-start.1 = ((f32[16,200,128]{2,1,0:T(8,128)}), f32[16,200,128]{2,1,0:T(8,128)S(1)}, u32[]{:S(2)}, u32[]{:S(2)}) async-start(f32[16,200,128]{2,1,0:T(8,128)} %get-tuple-element.34), calls=%async_computation.1 | async-start | bytes 3276800 | tf_op jit(solution)/shard_map/all_to_all | solution.py:409
  35.0 0.0 copy-done.1
  35.0 3.1 %collective-permute-start.2 = (f32[2,128,768]{2,1,0:T(8,128)S(1)}, f32[2,128,768]{2,1,0:T(8,128)S(1)}, u32[]{:S(2)}, u32[]{:S(2)}) collective-permute-start(f32[2,128,768]{2,1,0:T(8,128)S(1)} %copy-done.1), channel_id=1, source_target_pairs={{0,8},{4,12},{8,0},{12,4},{1,9},{5,13},{9,1},{13,5},{2,10},{6,14},... | collective-permute-start | bytes 2359304 | tf_op jit(solution)/shard_map/ppermute | solution.py:412
  38.1 16.9 %shard_map.30 = (f32[512,512]{1,0:T(8,128)}, f32[512,512]{1,0:T(8,128)}) custom-call(f32[16,72,128]{2,1,0:T(8,128)} %all_to_all.10.got), custom_call_target="tpu_custom_call" | custom-call | tf_op jit(solution)/shard_map/pallas_call | solution.py:410
  55.0 1.4 %collective-permute-start.1 = (f32[2,128,768]{2,1,0:T(8,128)S(1)}, f32[2,128,768]{2,1,0:T(8,128)}, u32[]{:S(2)}, u32[]{:S(2)}) collective-permute-start(f32[2,128,768]{2,1,0:T(8,128)S(1)} %copy-done.1), channel_id=1, source_target_pairs={{0,12},{4,0},{8,4},{12,8},{1,13},{5,1},{9,5},{13,9},{2,14},{6,2},{... | collective-permute-start | bytes 2359304 | tf_op jit(solution)/shard_map/ppermute | solution.py:412
  56.4 0.9 collective-permute-start
  57.2 12.8 %all-to-all-done.1.got = f32[16,200,128]{2,1,0:T(8,128)S(1)} async-done(((f32[16,200,128]{2,1,0:T(8,128)}), f32[16,200,128]{2,1,0:T(8,128)S(1)}, u32[]{:S(2)}, u32[]{:S(2)}) %all-to-all-start.1) | async-done | bytes 1638432 | tf_op jit(solution)/shard_map/all_to_all | solution.py:409
  70.1 1.2 copy-done
  71.2 19.3 %shard_map.31 = (f32[512,512]{1,0:T(8,128)}, f32[512,512]{1,0:T(8,128)}, f32[512,512]{1,0:T(8,128)}) custom-call(f32[16,200,128]{2,1,0:T(8,128)} %copy-done, f32[512,512]{1,0:T(8,128)} %get-tuple-element.33.inverse0.inv0), custom_call_target="tpu_custom_call" | custom-call | tf_op jit(solution)/shard_map/pallas_call | solution.py:414
  90.6 0.0 all-gather.3.cloned.1.call-done
  90.6 7.8 %shard_map.32 = (bf16[2,768,512]{2,1,0:T(8,128)(2,1)}, bf16[2,768,512]{2,1,0:T(8,128)(2,1)}, f32[2,768,128]{2,1,0:T(8,128)}) custom-call(f32[4,2,6,128,128]{4,3,2,1,0:T(8,128)} %bitcast.8, s32[2,32,32]{2,1,0:T(8,128)} %pattern.3, f32[512,512]{1,0:T(8,128)} %get-tuple-element.33.inverse0.inv0, f32[512,512]{1,0:T(8,128)} %get-tuple-element.35.across, ...), custom_call_target="tpu_custom_call" | custom-call | tf_op jit(solution)/shard_map/pallas_call | solution.py:421
  98.4 0.0 collective-permute-done.2.ac2
  98.4 0.0 copy-start.2
  98.4 0.0 collective-permute-done.1.ac3
  98.4 0.0 collective-permute-done.ac1
  98.4 0.9 copy-done.2
  99.3 11.3 %shard_map.33 = f32[8,128,8,128]{3,2,1,0:T(8,128)} custom-call(f32[8,128,8,128]{3,2,1,0:T(8,128)} %bitcast.7, s32[2,32,32]{2,1,0:T(8,128)} %pattern.3, bf16[2,768,512]{2,1,0:T(8,128)(2,1)} %get-tuple-element.37.xh_in, bf16[2,768,512]{2,1,0:T(8,128)(2,1)} %get-tuple-element.38.xl_in, f32[2,768,128]{2,1,0:T(8,128)} %get-tuple-element.39.own_cols, ...), custom_call_target="tpu_custom_call" | custom-call | tf_op jit(solution)/shard_map/pallas_call | solution.py:428
  (2 shorter events, 0.0 us)
Async XLA Ops:
  6.5 84.1 %all-gather.3.cloned.1.call-start = ((), (), s32[]{:S(2)}) async-start(), calls=%async_computation.2 | async-start | bytes 3932160 | tf_op jit(solution)/shard_map/all_gather | solution.py:407
  9.2 2.7 %copy-start.3 = (f32[16,72,128]{2,1,0:T(8,128)S(1)}, f32[16,72,128]{2,1,0:T(8,128)}, u32[]{:S(2)}) copy-start(f32[16,72,128]{2,1,0:T(8,128)} %get-tuple-element.29) | copy-start | bytes 1769476
  29.2 5.8 %copy-start.1 = (f32[2,128,768]{2,1,0:T(8,128)S(1)}, f32[2,128,768]{2,1,0:T(8,128)}, u32[]{:S(2)}) copy-start(f32[2,128,768]{2,1,0:T(8,128)} %get-tuple-element.40.ac0) | copy-start | bytes 2359300
  29.2 40.9 %all-to-all-start.1 = ((f32[16,200,128]{2,1,0:T(8,128)}), f32[16,200,128]{2,1,0:T(8,128)S(1)}, u32[]{:S(2)}, u32[]{:S(2)}) async-start(f32[16,200,128]{2,1,0:T(8,128)} %get-tuple-element.34), calls=%async_computation.1 | async-start | bytes 3276800 | tf_op jit(solution)/shard_map/all_to_all | solution.py:409
  35.0 63.4 %collective-permute-start.2 = (f32[2,128,768]{2,1,0:T(8,128)S(1)}, f32[2,128,768]{2,1,0:T(8,128)S(1)}, u32[]{:S(2)}, u32[]{:S(2)}) collective-permute-start(f32[2,128,768]{2,1,0:T(8,128)S(1)} %copy-done.1), channel_id=1, source_target_pairs={{0,8},{4,12},{8,0},{12,4},{1,9},{5,13},{9,1},{13,5},{2,10},{6,14},... | collective-permute-start | bytes 2359304 | tf_op jit(solution)/shard_map/ppermute | solution.py:412
  55.0 43.5 %collective-permute-start.1 = (f32[2,128,768]{2,1,0:T(8,128)S(1)}, f32[2,128,768]{2,1,0:T(8,128)}, u32[]{:S(2)}, u32[]{:S(2)}) collective-permute-start(f32[2,128,768]{2,1,0:T(8,128)S(1)} %copy-done.1), channel_id=1, source_target_pairs={{0,12},{4,0},{8,4},{12,8},{1,13},{5,1},{9,5},{13,9},{2,14},{6,2},{... | collective-permute-start | bytes 2359304 | tf_op jit(solution)/shard_map/ppermute | solution.py:412
  56.4 42.1 %collective-permute-start = (f32[2,128,768]{2,1,0:T(8,128)S(1)}, f32[2,128,768]{2,1,0:T(8,128)}, u32[]{:S(2)}, u32[]{:S(2)}) collective-permute-start(f32[2,128,768]{2,1,0:T(8,128)S(1)} %copy-done.1), channel_id=1, source_target_pairs={{0,4},{4,8},{8,12},{12,0},{1,5},{5,9},{9,13},{13,1},{2,6},{6,10},{... | collective-permute-start | bytes 2359304 | tf_op jit(solution)/shard_map/ppermute | solution.py:412
  70.1 1.2 copy-start
  98.4 0.9 copy-start.2
Sparse Core Ops, SparseCore 0:
  11.9 60.3 all-gather.2

commit v3 on v2

--- a/solution.py
+++ b/solution.py
@@ -269,7 +269,7 @@
     copies = [pltpu.make_async_copy(*pair, arrive.at[8 + i])
               for i, pair in enumerate(((own_cols, held), (xh_in, xh), (xl_in, xl)))]
     fronts = [pltpu.make_async_copy(front.at[l], buf.at[l], arrive.at[16 + l]) for l in range(NPAN, LB)]
-    for load in loads[0] + loads[1] + copies + fronts:
+    for load in loads[0] + loads[1]:
         load.start()
     zero = jnp.zeros((EDGE, EDGE), F32)
     for l in range(NPAN):
@@ -310,6 +310,9 @@
     for k in range(NPAN):
         for load in loads[k]:
             load.wait()
+        if k == 0:
+            for load in copies + fronts:
+                load.start()
         if k == 1:
             visit(ids, 0, col_end, col_product, col_target)
         for g in range(GROUPS):
@@ -405,12 +408,11 @@
         in_specs=[away], out_specs=[away, away],
     )(later)
     ar = lax.all_gather(ar, "col", axis=0)
-    c1, ac, got0 = lax.optimization_barrier((c1, ac, got0))
+    c1, got0 = lax.optimization_barrier((c1, got0))
     got1 = lax.all_to_all(c1, ("row", "col"), 0, 0, tiled=True)
     low0, inv0 = call(first_kernel, [square] * 2, work, out_specs=[away] * 2)(got0)
-    later, inv0 = lax.optimization_barrier((ac, inv0))
-    acs = [ac] + [lax.ppermute(piece, "row", [(i, (i + s) % GROUPS) for i in range(GROUPS)])
-                  for s, piece in ((1, later), (3, later), (2, ac))]
+    ac, got1, inv0 = lax.optimization_barrier((ac, got1, inv0))
+    acs = [ac] + [lax.ppermute(ac, "row", [(i, (i + s) % GROUPS) for i in range(GROUPS)]) for s in (1, 3, 2)]
     across, low1, inv1 = call(
         second_kernel, [square] * 3,
         work + [vmem(every, EDGE, EDGE), vmem(every, HELD, EDGE), vmem(WIDTH, WIDTH), vmem(WIDTH, WIDTH), dma((4,))],

time: 119 us -> 117 us (0.983)
  local copies, waits for them, and re-layouts: 2.05 us -> 0.02 us
  Pallas kernels: 60.5 us -> 62.3 us
  waiting for transfers between devices: 12.9 us -> 11.6 us
    all_to_all x1, waiting for transfers between devices: 12.8 us -> 7.08 us  [per_device(): got1 = lax.all_to_all(c1, ('row', 'col'), 0, 0, tiled=True)]
    ppermute x3, waiting for transfers between devices: 0.01 us -> 4.45 us  [per_device(): lax.ppermute(ac, 'row', [(i, (i + s) % GROUPS) for i in range(GROUPS)])]
    unnamed x8, local copies, waits for them, and re-layouts: 2.05 us -> 0.02 us
  transfers between devices with their start and end apart: 5 -> 5, of which waited for: 1 -> 2; matrix products, arithmetic and copies ran while one was open for 0% -> 0% of each run, Pallas kernels for 37% -> 39%
where the time goes in v3:
time: 117 us; the launch traced here: 115 us
  Pallas kernels  62.3 us (53%)
  blocking collectives  17.4 us (15%)
  between operations  13.5 us (12%)
  waiting for transfers between devices  11.6 us (10%)
  starting transfers between devices  10.1 us (9%)
    pallas_call x1, Pallas kernels, per_device(): call(second_kernel, [square] * 3, work + [vmem(every, EDGE, EDGE), vmem(e...  19.4 us
    all_to_all x1, blocking collectives, per_device(): got0 = lax.all_to_all(c0, ('row', 'col'), 0, 0, tiled=True)  17.4 us
    pallas_call x1, Pallas kernels, per_device(): call(first_kernel, [square] * 2, work, out_specs=[away] * 2)(got0)  16.9 us
    pallas_call x1, Pallas kernels, per_device(): call(last_kernel, shape(LB, EDGE, LB, EDGE), [vmem(LB, EDGE, LB, EDGE), v...  12.5 us
    pallas_call x1, Pallas kernels, per_device(): call(row_kernel, [jax.ShapeDtypeStruct(dims, BF16) for dims in tall] + [s...  8.37 us
    all_to_all x1, waiting for transfers between devices, per_device(): got1 = lax.all_to_all(c1, ('row', 'col'), 0, 0, tiled=True)  7.08 us
    all_to_all x1, starting transfers between devices, per_device(): got1 = lax.all_to_all(c1, ('row', 'col'), 0, 0, tiled=True)  5.78 us
    ppermute x3, waiting for transfers between devices, per_device(): lax.ppermute(ac, 'row', [(i, (i + s) % GROUPS) for i in range(GROUPS)])  4.45 us
  transfers between devices with their start and end apart: 5, of which 2 were waited for; matrix products, arithmetic and copies ran while one was open for 0% of the time, Pallas kernels for 39%

profile of v3, /device:TPU:112, one launch (start us, length us, event | category | flops | bytes accessed | tf_op | source)
XLA Modules:
  0.0 114.8 jit_solution(11776274704263462753)
XLA Ops:
  6.5 0.0 all-gather.3.cloned.1.call-start
  6.5 2.6 %shard_map.28 = (f32[16,72,128]{2,1,0:T(8,128)}, f32[16,200,128]{2,1,0:T(8,128)}) custom-call(f32[8,128,8,128]{3,2,1,0:T(8,128)} %bitcast.5), custom_call_target="tpu_custom_call" | custom-call | tf_op jit(solution)/shard_map/pallas_call | solution.py:398
  9.2 0.0 copy-start.3
  9.2 2.6 %shard_map.29 = (f32[2,6,128,128]{3,2,1,0:T(8,128)}, f32[2,128,768]{2,1,0:T(8,128)}) custom-call(f32[8,128,8,128]{3,2,1,0:T(8,128)} %bitcast.6), custom_call_target="tpu_custom_call" | custom-call | tf_op jit(solution)/shard_map/pallas_call | solution.py:405
  11.8 0.0 all-gather.3.cloned.1.call-update
  11.8 0.0 copy-done.3
  11.8 17.4 %all_to_all.10.got = f32[16,72,128]{2,1,0:T(8,128)} all-to-all(f32[16,72,128]{2,1,0:T(8,128)S(1)} %copy-done.3), channel_id=1, replica_groups=mesh['front'=16,'row'=4,'col'=4] {'row','col'}, dimensions={0} | all-to-all | bytes 1179648 | tf_op jit(solution)/shard_map/all_to_all | solution.py:404
  29.2 5.8 %all-to-all-start.1 = ((f32[16,200,128]{2,1,0:T(8,128)}), f32[16,200,128]{2,1,0:T(8,128)S(1)}, u32[]{:S(2)}, u32[]{:S(2)}) async-start(f32[16,200,128]{2,1,0:T(8,128)} %get-tuple-element.30), calls=%async_computation.1 | async-start | bytes 3276800 | tf_op jit(solution)/shard_map/all_to_all | solution.py:412
  35.0 16.9 %shard_map.30 = (f32[512,512]{1,0:T(8,128)}, f32[512,512]{1,0:T(8,128)}) custom-call(f32[16,72,128]{2,1,0:T(8,128)} %all_to_all.10.got), custom_call_target="tpu_custom_call" | custom-call | tf_op jit(solution)/shard_map/pallas_call | solution.py:413
  51.8 7.1 %all-to-all-done.1.got = f32[16,200,128]{2,1,0:T(8,128)S(1)} async-done(((f32[16,200,128]{2,1,0:T(8,128)}), f32[16,200,128]{2,1,0:T(8,128)S(1)}, u32[]{:S(2)}, u32[]{:S(2)}) %all-to-all-start.1) | async-done | bytes 1638432 | tf_op jit(solution)/shard_map/all_to_all | solution.py:412
  58.9 0.0 copy-done.1
  58.9 2.3 %collective-permute-start.2 = (f32[2,128,768]{2,1,0:T(8,128)S(1)}, f32[2,128,768]{2,1,0:T(8,128)S(1)}, u32[]{:S(2)}, u32[]{:S(2)}) collective-permute-start(f32[2,128,768]{2,1,0:T(8,128)S(1)} %copy-done.1), channel_id=1, source_target_pairs={{0,8},{4,12},{8,0},{12,4},{1,9},{5,13},{9,1},{13,5},{2,10},{6,14},... | collective-permute-start | bytes 2359304 | tf_op jit(solution)/shard_map/ppermute | solution.py:415
  61.2 1.1 collective-permute-start.1
  62.3 0.9 collective-permute-start
  63.2 0.0 copy-done
  63.2 19.4 %shard_map.31 = (f32[512,512]{1,0:T(8,128)}, f32[512,512]{1,0:T(8,128)}, f32[512,512]{1,0:T(8,128)}) custom-call(f32[16,200,128]{2,1,0:T(8,128)} %copy-done, f32[512,512]{1,0:T(8,128)} %get-tuple-element.33.inverse0.inv0), custom_call_target="tpu_custom_call" | custom-call | tf_op jit(solution)/shard_map/pallas_call | solution.py:416
  82.6 0.0 all-gather.3.cloned.1.call-done
  82.6 8.4 %shard_map.32 = (bf16[2,768,512]{2,1,0:T(8,128)(2,1)}, bf16[2,768,512]{2,1,0:T(8,128)(2,1)}, f32[2,768,128]{2,1,0:T(8,128)}) custom-call(f32[4,2,6,128,128]{4,3,2,1,0:T(8,128)} %bitcast.8, s32[2,32,32]{2,1,0:T(8,128)} %pattern.3, f32[512,512]{1,0:T(8,128)} %get-tuple-element.33.inverse0.inv0, f32[512,512]{1,0:T(8,128)} %get-tuple-element.35.across, ...), custom_call_target="tpu_custom_call" | custom-call | tf_op jit(solution)/shard_map/pallas_call | solution.py:423
  91.0 0.0 collective-permute-done.2.ac2
  91.0 0.0 copy-start.2
  91.0 4.4 %collective-permute-done.1.ac3 = f32[2,128,768]{2,1,0:T(8,128)} collective-permute-done((f32[2,128,768]{2,1,0:T(8,128)S(1)}, f32[2,128,768]{2,1,0:T(8,128)}, u32[]{:S(2)}, u32[]{:S(2)}) %collective-permute-start.1) | collective-permute-done | bytes 786464 | tf_op jit(solution)/shard_map/ppermute | solution.py:415
  95.5 0.0 collective-permute-done.ac1
  95.5 0.0 copy-done.2
  95.5 12.5 %shard_map.33 = f32[8,128,8,128]{3,2,1,0:T(8,128)} custom-call(f32[8,128,8,128]{3,2,1,0:T(8,128)} %bitcast.7, s32[2,32,32]{2,1,0:T(8,128)} %pattern.3, bf16[2,768,512]{2,1,0:T(8,128)(2,1)} %get-tuple-element.37.xh_in, bf16[2,768,512]{2,1,0:T(8,128)(2,1)} %get-tuple-element.38.xl_in, f32[2,768,128]{2,1,0:T(8,128)} %get-tuple-element.39.own_cols, ...), custom_call_target="tpu_custom_call" | custom-call | tf_op jit(solution)/shard_map/pallas_call | solution.py:430
  (2 shorter events, 0.0 us)
Async XLA Ops:
  6.5 76.1 %all-gather.3.cloned.1.call-start = ((), (), s32[]{:S(2)}) async-start(), calls=%async_computation.2 | async-start | bytes 3932160 | tf_op jit(solution)/shard_map/all_gather | solution.py:410
  9.2 2.7 %copy-start.3 = (f32[16,72,128]{2,1,0:T(8,128)S(1)}, f32[16,72,128]{2,1,0:T(8,128)}, u32[]{:S(2)}) copy-start(f32[16,72,128]{2,1,0:T(8,128)} %get-tuple-element.29) | copy-start | bytes 1769476
  29.2 29.8 %copy-start.1 = (f32[2,128,768]{2,1,0:T(8,128)S(1)}, f32[2,128,768]{2,1,0:T(8,128)}, u32[]{:S(2)}) copy-start(f32[2,128,768]{2,1,0:T(8,128)} %get-tuple-element.40.ac0) | copy-start | bytes 2359300
  29.2 29.7 %all-to-all-start.1 = ((f32[16,200,128]{2,1,0:T(8,128)}), f32[16,200,128]{2,1,0:T(8,128)S(1)}, u32[]{:S(2)}, u32[]{:S(2)}) async-start(f32[16,200,128]{2,1,0:T(8,128)} %get-tuple-element.30), calls=%async_computation.1 | async-start | bytes 3276800 | tf_op jit(solution)/shard_map/all_to_all | solution.py:412
  58.9 4.3 %copy-start = (f32[16,200,128]{2,1,0:T(8,128)}, f32[16,200,128]{2,1,0:T(8,128)S(1)}, u32[]{:S(2)}) copy-start(f32[16,200,128]{2,1,0:T(8,128)S(1)} %all-to-all-done.1.got) | copy-start | bytes 4915204
  58.9 32.1 %collective-permute-start.2 = (f32[2,128,768]{2,1,0:T(8,128)S(1)}, f32[2,128,768]{2,1,0:T(8,128)S(1)}, u32[]{:S(2)}, u32[]{:S(2)}) collective-permute-start(f32[2,128,768]{2,1,0:T(8,128)S(1)} %copy-done.1), channel_id=1, source_target_pairs={{0,8},{4,12},{8,0},{12,4},{1,9},{5,13},{9,1},{13,5},{2,10},{6,14},... | collective-permute-start | bytes 2359304 | tf_op jit(solution)/shard_map/ppermute | solution.py:415
  61.2 34.3 %collective-permute-start.1 = (f32[2,128,768]{2,1,0:T(8,128)S(1)}, f32[2,128,768]{2,1,0:T(8,128)}, u32[]{:S(2)}, u32[]{:S(2)}) collective-permute-start(f32[2,128,768]{2,1,0:T(8,128)S(1)} %copy-done.1), channel_id=1, source_target_pairs={{0,12},{4,0},{8,4},{12,8},{1,13},{5,1},{9,5},{13,9},{2,14},{6,2},{... | collective-permute-start | bytes 2359304 | tf_op jit(solution)/shard_map/ppermute | solution.py:415
  62.3 33.2 %collective-permute-start = (f32[2,128,768]{2,1,0:T(8,128)S(1)}, f32[2,128,768]{2,1,0:T(8,128)}, u32[]{:S(2)}, u32[]{:S(2)}) collective-permute-start(f32[2,128,768]{2,1,0:T(8,128)S(1)} %copy-done.1), channel_id=1, source_target_pairs={{0,4},{4,8},{8,12},{12,0},{1,5},{5,9},{9,13},{13,1},{2,6},{6,10},{... | collective-permute-start | bytes 2359304 | tf_op jit(solution)/shard_map/ppermute | solution.py:415
  91.0 4.5 %copy-start.2 = (f32[2,128,768]{2,1,0:T(8,128)}, f32[2,128,768]{2,1,0:T(8,128)S(1)}, u32[]{:S(2)}) copy-start(f32[2,128,768]{2,1,0:T(8,128)S(1)} %collective-permute-done.2.ac2) | copy-start | bytes 2359300
Sparse Core Ops, SparseCore 0:
  11.9 60.3 all-gather.2

commit v4 on v2

--- a/solution.py
+++ b/solution.py
@@ -408,9 +408,9 @@
     c1, ac, got0 = lax.optimization_barrier((c1, ac, got0))
     got1 = lax.all_to_all(c1, ("row", "col"), 0, 0, tiled=True)
     low0, inv0 = call(first_kernel, [square] * 2, work, out_specs=[away] * 2)(got0)
-    later, inv0 = lax.optimization_barrier((ac, inv0))
+    later, got1, inv0 = lax.optimization_barrier((ac, got1, inv0))
     acs = [ac] + [lax.ppermute(piece, "row", [(i, (i + s) % GROUPS) for i in range(GROUPS)])
-                  for s, piece in ((1, later), (3, later), (2, ac))]
+                  for s, piece in ((1, ac), (3, later), (2, later))]
     across, low1, inv1 = call(
         second_kernel, [square] * 3,
         work + [vmem(every, EDGE, EDGE), vmem(every, HELD, EDGE), vmem(WIDTH, WIDTH), vmem(WIDTH, WIDTH), dma((4,))],

time: 119 us -> 116 us (0.975)
  local copies, waits for them, and re-layouts: 2.05 us -> 0.02 us
  waiting for transfers between devices: 12.9 us -> 10.9 us
  Pallas kernels: 60.5 us -> 61.7 us
    all_to_all x1, waiting for transfers between devices: 12.8 us -> 5.51 us  [per_device(): got1 = lax.all_to_all(c1, ('row', 'col'), 0, 0, tiled=True)]
    ppermute x3, waiting for transfers between devices: 0.01 us -> 5.34 us  [per_device(): lax.ppermute(piece, 'row', [(i, (i + s) % GROUPS) for i in range(GROUPS)])]
    unnamed x8, local copies, waits for them, and re-layouts: 2.05 us -> 0.02 us
  transfers between devices with their start and end apart: 5 -> 5, of which waited for: 1 -> 2; matrix products, arithmetic and copies ran while one was open for 0% -> 0% of each run, Pallas kernels for 37% -> 39%
where the time goes in v4:
time: 116 us; the launch traced here: 114 us
  Pallas kernels  61.7 us (53%)
  blocking collectives  17.4 us (15%)
  between operations  13.5 us (12%)
  waiting for transfers between devices  10.9 us (9%)
  starting transfers between devices  10.7 us (9%)
    pallas_call x1, Pallas kernels, per_device(): call(second_kernel, [square] * 3, work + [vmem(every, EDGE, EDGE), vmem(e...  19.4 us
    all_to_all x1, blocking collectives, per_device(): got0 = lax.all_to_all(c0, ('row', 'col'), 0, 0, tiled=True)  17.4 us
    pallas_call x1, Pallas kernels, per_device(): call(first_kernel, [square] * 2, work, out_specs=[away] * 2)(got0)  16.9 us
    pallas_call x1, Pallas kernels, per_device(): call(last_kernel, shape(LB, EDGE, LB, EDGE), [vmem(LB, EDGE, LB, EDGE), v...  11.9 us
    pallas_call x1, Pallas kernels, per_device(): call(row_kernel, [jax.ShapeDtypeStruct(dims, BF16) for dims in tall] + [s...  8.36 us
    all_to_all x1, starting transfers between devices, per_device(): got1 = lax.all_to_all(c1, ('row', 'col'), 0, 0, tiled=True)  5.78 us
    all_to_all x1, waiting for transfers between devices, per_device(): got1 = lax.all_to_all(c1, ('row', 'col'), 0, 0, tiled=True)  5.51 us
    ppermute x3, waiting for transfers between devices, per_device(): lax.ppermute(piece, 'row', [(i, (i + s) % GROUPS) for i in range(GROUPS)])  5.34 us
  transfers between devices with their start and end apart: 5, of which 2 were waited for; matrix products, arithmetic and copies ran while one was open for 0% of the time, Pallas kernels for 39%

profile of v4, /device:TPU:112, one launch (start us, length us, event | category | flops | bytes accessed | tf_op | source)
XLA Modules:
  0.0 114.2 jit_solution(1887737646337356937)
XLA Ops:
  6.5 0.0 all-gather.3.cloned.1.call-start
  6.5 2.6 %shard_map.28 = (f32[16,72,128]{2,1,0:T(8,128)}, f32[16,200,128]{2,1,0:T(8,128)}) custom-call(f32[8,128,8,128]{3,2,1,0:T(8,128)} %bitcast.5), custom_call_target="tpu_custom_call" | custom-call | tf_op jit(solution)/shard_map/pallas_call | solution.py:395
  9.2 0.0 copy-start.3
  9.2 2.6 %shard_map.29 = (f32[2,6,128,128]{3,2,1,0:T(8,128)}, f32[2,128,768]{2,1,0:T(8,128)}) custom-call(f32[8,128,8,128]{3,2,1,0:T(8,128)} %bitcast.6), custom_call_target="tpu_custom_call" | custom-call | tf_op jit(solution)/shard_map/pallas_call | solution.py:402
  11.8 0.0 all-gather.3.cloned.1.call-update
  11.8 0.0 copy-done.3
  11.8 17.4 %all_to_all.10.got = f32[16,72,128]{2,1,0:T(8,128)} all-to-all(f32[16,72,128]{2,1,0:T(8,128)S(1)} %copy-done.3), channel_id=1, replica_groups=mesh['front'=16,'row'=4,'col'=4] {'row','col'}, dimensions={0} | all-to-all | bytes 1179648 | tf_op jit(solution)/shard_map/all_to_all | solution.py:401
  29.2 5.8 %all-to-all-start.1 = ((f32[16,200,128]{2,1,0:T(8,128)}), f32[16,200,128]{2,1,0:T(8,128)S(1)}, u32[]{:S(2)}, u32[]{:S(2)}) async-start(f32[16,200,128]{2,1,0:T(8,128)} %get-tuple-element.32), calls=%async_computation.1 | async-start | bytes 3276800 | tf_op jit(solution)/shard_map/all_to_all | solution.py:409
  35.0 0.0 copy-done.1
  35.0 1.6 %collective-permute-start = (f32[2,128,768]{2,1,0:T(8,128)S(1)}, f32[2,128,768]{2,1,0:T(8,128)S(1)}, u32[]{:S(2)}, u32[]{:S(2)}) collective-permute-start(f32[2,128,768]{2,1,0:T(8,128)S(1)} %copy-done.1), channel_id=1, source_target_pairs={{0,4},{4,8},{8,12},{12,0},{1,5},{5,9},{9,13},{13,1},{2,6},{6,10},{... | collective-permute-start | bytes 2359304 | tf_op jit(solution)/shard_map/ppermute | solution.py:412
  36.5 16.9 %shard_map.30 = (f32[512,512]{1,0:T(8,128)}, f32[512,512]{1,0:T(8,128)}) custom-call(f32[16,72,128]{2,1,0:T(8,128)} %all_to_all.10.got), custom_call_target="tpu_custom_call" | custom-call | tf_op jit(solution)/shard_map/pallas_call | solution.py:410
  53.4 5.5 %all-to-all-done.1.got = f32[16,200,128]{2,1,0:T(8,128)S(1)} async-done(((f32[16,200,128]{2,1,0:T(8,128)}), f32[16,200,128]{2,1,0:T(8,128)S(1)}, u32[]{:S(2)}, u32[]{:S(2)}) %all-to-all-start.1) | async-done | bytes 1638432 | tf_op jit(solution)/shard_map/all_to_all | solution.py:409
  58.9 2.3 %collective-permute-start.2 = (f32[2,128,768]{2,1,0:T(8,128)S(1)}, f32[2,128,768]{2,1,0:T(8,128)}, u32[]{:S(2)}, u32[]{:S(2)}) collective-permute-start(f32[2,128,768]{2,1,0:T(8,128)S(1)} %copy-done.1), channel_id=1, source_target_pairs={{0,8},{4,12},{8,0},{12,4},{1,9},{5,13},{9,1},{13,5},{2,10},{6,14},... | collective-permute-start | bytes 2359304 | tf_op jit(solution)/shard_map/ppermute | solution.py:412
  61.2 1.1 collective-permute-start.1
  62.3 0.0 copy-done
  62.3 19.4 %shard_map.31 = (f32[512,512]{1,0:T(8,128)}, f32[512,512]{1,0:T(8,128)}, f32[512,512]{1,0:T(8,128)}) custom-call(f32[16,200,128]{2,1,0:T(8,128)} %copy-done, f32[512,512]{1,0:T(8,128)} %get-tuple-element.35.inverse0.inv0), custom_call_target="tpu_custom_call" | custom-call | tf_op jit(solution)/shard_map/pallas_call | solution.py:414
  81.7 0.0 all-gather.3.cloned.1.call-done
  81.7 8.4 %shard_map.32 = (bf16[2,768,512]{2,1,0:T(8,128)(2,1)}, bf16[2,768,512]{2,1,0:T(8,128)(2,1)}, f32[2,768,128]{2,1,0:T(8,128)}) custom-call(f32[4,2,6,128,128]{4,3,2,1,0:T(8,128)} %bitcast.8, s32[2,32,32]{2,1,0:T(8,128)} %pattern.3, f32[512,512]{1,0:T(8,128)} %get-tuple-element.35.inverse0.inv0, f32[512,512]{1,0:T(8,128)} %get-tuple-element.37.across, ...), custom_call_target="tpu_custom_call" | custom-call | tf_op jit(solution)/shard_map/pallas_call | solution.py:421
  90.1 0.0 collective-permute-done.ac1
  90.1 0.0 copy-start.2
  90.1 0.0 collective-permute-done.2.ac2
  90.1 5.3 %collective-permute-done.1.ac3 = f32[2,128,768]{2,1,0:T(8,128)} collective-permute-done((f32[2,128,768]{2,1,0:T(8,128)S(1)}, f32[2,128,768]{2,1,0:T(8,128)}, u32[]{:S(2)}, u32[]{:S(2)}) %collective-permute-start.1) | collective-permute-done | bytes 786464 | tf_op jit(solution)/shard_map/ppermute | solution.py:412
  95.5 0.0 copy-done.2
  95.5 11.9 %shard_map.33 = f32[8,128,8,128]{3,2,1,0:T(8,128)} custom-call(f32[8,128,8,128]{3,2,1,0:T(8,128)} %bitcast.7, s32[2,32,32]{2,1,0:T(8,128)} %pattern.3, bf16[2,768,512]{2,1,0:T(8,128)(2,1)} %get-tuple-element.39.xh_in, bf16[2,768,512]{2,1,0:T(8,128)(2,1)} %get-tuple-element.40.xl_in, f32[2,768,128]{2,1,0:T(8,128)} %get-tuple-element.41.own_cols, ...), custom_call_target="tpu_custom_call" | custom-call | tf_op jit(solution)/shard_map/pallas_call | solution.py:428
  (2 shorter events, 0.0 us)
Async XLA Ops:
  6.5 75.2 %all-gather.3.cloned.1.call-start = ((), (), s32[]{:S(2)}) async-start(), calls=%async_computation.2 | async-start | bytes 3932160 | tf_op jit(solution)/shard_map/all_gather | solution.py:407
  9.2 2.7 %copy-start.3 = (f32[16,72,128]{2,1,0:T(8,128)S(1)}, f32[16,72,128]{2,1,0:T(8,128)}, u32[]{:S(2)}) copy-start(f32[16,72,128]{2,1,0:T(8,128)} %get-tuple-element.30) | copy-start | bytes 1769476
  29.2 5.8 %copy-start.1 = (f32[2,128,768]{2,1,0:T(8,128)S(1)}, f32[2,128,768]{2,1,0:T(8,128)}, u32[]{:S(2)}) copy-start(f32[2,128,768]{2,1,0:T(8,128)} %get-tuple-element.42.ac0) | copy-start | bytes 2359300
  29.2 29.7 %all-to-all-start.1 = ((f32[16,200,128]{2,1,0:T(8,128)}), f32[16,200,128]{2,1,0:T(8,128)S(1)}, u32[]{:S(2)}, u32[]{:S(2)}) async-start(f32[16,200,128]{2,1,0:T(8,128)} %get-tuple-element.32), calls=%async_computation.1 | async-start | bytes 3276800 | tf_op jit(solution)/shard_map/all_to_all | solution.py:409
  35.0 55.1 %collective-permute-start = (f32[2,128,768]{2,1,0:T(8,128)S(1)}, f32[2,128,768]{2,1,0:T(8,128)S(1)}, u32[]{:S(2)}, u32[]{:S(2)}) collective-permute-start(f32[2,128,768]{2,1,0:T(8,128)S(1)} %copy-done.1), channel_id=1, source_target_pairs={{0,4},{4,8},{8,12},{12,0},{1,5},{5,9},{9,13},{13,1},{2,6},{6,10},{... | collective-permute-start | bytes 2359304 | tf_op jit(solution)/shard_map/ppermute | solution.py:412
  58.9 3.4 %copy-start = (f32[16,200,128]{2,1,0:T(8,128)}, f32[16,200,128]{2,1,0:T(8,128)S(1)}, u32[]{:S(2)}) copy-start(f32[16,200,128]{2,1,0:T(8,128)S(1)} %all-to-all-done.1.got) | copy-start | bytes 4915204
  58.9 31.2 %collective-permute-start.2 = (f32[2,128,768]{2,1,0:T(8,128)S(1)}, f32[2,128,768]{2,1,0:T(8,128)}, u32[]{:S(2)}, u32[]{:S(2)}) collective-permute-start(f32[2,128,768]{2,1,0:T(8,128)S(1)} %copy-done.1), channel_id=1, source_target_pairs={{0,8},{4,12},{8,0},{12,4},{1,9},{5,13},{9,1},{13,5},{2,10},{6,14},... | collective-permute-start | bytes 2359304 | tf_op jit(solution)/shard_map/ppermute | solution.py:412
  61.2 34.3 %collective-permute-start.1 = (f32[2,128,768]{2,1,0:T(8,128)S(1)}, f32[2,128,768]{2,1,0:T(8,128)}, u32[]{:S(2)}, u32[]{:S(2)}) collective-permute-start(f32[2,128,768]{2,1,0:T(8,128)S(1)} %copy-done.1), channel_id=1, source_target_pairs={{0,12},{4,0},{8,4},{12,8},{1,13},{5,1},{9,5},{13,9},{2,14},{6,2},{... | collective-permute-start | bytes 2359304 | tf_op jit(solution)/shard_map/ppermute | solution.py:412
  90.1 5.4 %copy-start.2 = (f32[2,128,768]{2,1,0:T(8,128)}, f32[2,128,768]{2,1,0:T(8,128)S(1)}, u32[]{:S(2)}) copy-start(f32[2,128,768]{2,1,0:T(8,128)S(1)} %collective-permute-done.ac1) | copy-start | bytes 2359300
Sparse Core Ops, SparseCore 0:
  11.9 60.3 all-gather.2

commit v5 on v2

--- a/solution.py
+++ b/solution.py
@@ -405,12 +405,12 @@
         in_specs=[away], out_specs=[away, away],
     )(later)
     ar = lax.all_gather(ar, "col", axis=0)
-    c1, ac, got0 = lax.optimization_barrier((c1, ac, got0))
+    c1, got0 = lax.optimization_barrier((c1, got0))
     got1 = lax.all_to_all(c1, ("row", "col"), 0, 0, tiled=True)
     low0, inv0 = call(first_kernel, [square] * 2, work, out_specs=[away] * 2)(got0)
     later, inv0 = lax.optimization_barrier((ac, inv0))
     acs = [ac] + [lax.ppermute(piece, "row", [(i, (i + s) % GROUPS) for i in range(GROUPS)])
-                  for s, piece in ((1, later), (3, later), (2, ac))]
+                  for s, piece in ((1, later), (3, later), (2, later))]
     across, low1, inv1 = call(
         second_kernel, [square] * 3,
         work + [vmem(every, EDGE, EDGE), vmem(every, HELD, EDGE), vmem(WIDTH, WIDTH), vmem(WIDTH, WIDTH), dma((4,))],

time: 119 us -> 119 us (level)
    pallas_call x1, Pallas kernels: 11.3 us -> 9.97 us  [per_device(): call(last_kernel, shape(LB, EDGE, LB, EDGE), [vmem(LB, EDGE, LB, EDGE), v...]
  transfers between devices with their start and end apart: 5 -> 5, of which waited for: 1 -> 1; matrix products, arithmetic and copies ran while one was open for 0% -> 0% of each run, Pallas kernels for 37% -> 38%
where the time goes in v5:
time: 119 us; the launch traced here: 117 us
  Pallas kernels  59.8 us (50%)
  blocking collectives  17.4 us (15%)
  waiting for transfers between devices  13.6 us (11%)
  between operations  13.5 us (11%)
  starting transfers between devices  10.9 us (9%)
  local copies, waits for them, and re-layouts  2.05 us (2%)
    pallas_call x1, Pallas kernels, per_device(): call(second_kernel, [square] * 3, work + [vmem(every, EDGE, EDGE), vmem(e...  19.3 us
    all_to_all x1, blocking collectives, per_device(): got0 = lax.all_to_all(c0, ('row', 'col'), 0, 0, tiled=True)  17.4 us
    pallas_call x1, Pallas kernels, per_device(): call(first_kernel, [square] * 2, work, out_specs=[away] * 2)(got0)  16.9 us
    all_to_all x1, waiting for transfers between devices, per_device(): got1 = lax.all_to_all(c1, ('row', 'col'), 0, 0, tiled=True)  13.5 us
    pallas_call x1, Pallas kernels, per_device(): call(last_kernel, shape(LB, EDGE, LB, EDGE), [vmem(LB, EDGE, LB, EDGE), v...  9.97 us
    pallas_call x1, Pallas kernels, per_device(): call(row_kernel, [jax.ShapeDtypeStruct(dims, BF16) for dims in tall] + [s...  8.36 us
    all_to_all x1, starting transfers between devices, per_device(): got1 = lax.all_to_all(c1, ('row', 'col'), 0, 0, tiled=True)  5.78 us
    ppermute x3, starting transfers between devices, per_device(): lax.ppermute(piece, 'row', [(i, (i + s) % GROUPS) for i in range(GROUPS)])  5.13 us
  transfers between devices with their start and end apart: 5, of which 1 were waited for; matrix products, arithmetic and copies ran while one was open for 0% of the time, Pallas kernels for 38%

profile of v5, /device:TPU:112, one launch (start us, length us, event | category | flops | bytes accessed | tf_op | source)
XLA Modules:
  0.0 117.2 jit_solution(11530005011827880269)
XLA Ops:
  6.5 0.0 all-gather.3.cloned.1.call-start
  6.5 2.6 %shard_map.28 = (f32[16,72,128]{2,1,0:T(8,128)}, f32[16,200,128]{2,1,0:T(8,128)}) custom-call(f32[8,128,8,128]{3,2,1,0:T(8,128)} %bitcast.5), custom_call_target="tpu_custom_call" | custom-call | tf_op jit(solution)/shard_map/pallas_call | solution.py:395
  9.2 0.0 copy-start.3
  9.2 2.6 %shard_map.29 = (f32[2,6,128,128]{3,2,1,0:T(8,128)}, f32[2,128,768]{2,1,0:T(8,128)}) custom-call(f32[8,128,8,128]{3,2,1,0:T(8,128)} %bitcast.6), custom_call_target="tpu_custom_call" | custom-call | tf_op jit(solution)/shard_map/pallas_call | solution.py:402
  11.8 0.0 all-gather.3.cloned.1.call-update
  11.8 0.0 copy-done.3
  11.8 17.4 %all_to_all.10.got = f32[16,72,128]{2,1,0:T(8,128)} all-to-all(f32[16,72,128]{2,1,0:T(8,128)S(1)} %copy-done.3), channel_id=1, replica_groups=mesh['front'=16,'row'=4,'col'=4] {'row','col'}, dimensions={0} | all-to-all | bytes 1179648 | tf_op jit(solution)/shard_map/all_to_all | solution.py:401
  29.2 5.8 %all-to-all-start.1 = ((f32[16,200,128]{2,1,0:T(8,128)}), f32[16,200,128]{2,1,0:T(8,128)S(1)}, u32[]{:S(2)}, u32[]{:S(2)}) async-start(f32[16,200,128]{2,1,0:T(8,128)} %get-tuple-element.32), calls=%async_computation.1 | async-start | bytes 3276800 | tf_op jit(solution)/shard_map/all_to_all | solution.py:409
  35.0 16.9 %shard_map.30 = (f32[512,512]{1,0:T(8,128)}, f32[512,512]{1,0:T(8,128)}) custom-call(f32[16,72,128]{2,1,0:T(8,128)} %all_to_all.10.got), custom_call_target="tpu_custom_call" | custom-call | tf_op jit(solution)/shard_map/pallas_call | solution.py:410
  51.8 0.0 copy-done.1
  51.9 3.1 %collective-permute-start.2 = (f32[2,128,768]{2,1,0:T(8,128)S(1)}, f32[2,128,768]{2,1,0:T(8,128)S(1)}, u32[]{:S(2)}, u32[]{:S(2)}) collective-permute-start(f32[2,128,768]{2,1,0:T(8,128)S(1)} %copy-done.1), channel_id=1, source_target_pairs={{0,8},{4,12},{8,0},{12,4},{1,9},{5,13},{9,1},{13,5},{2,10},{6,14},... | collective-permute-start | bytes 2359304 | tf_op jit(solution)/shard_map/ppermute | solution.py:412
  55.0 1.1 collective-permute-start.1
  56.1 0.9 collective-permute-start
  57.0 13.5 %all-to-all-done.1.got = f32[16,200,128]{2,1,0:T(8,128)S(1)} async-done(((f32[16,200,128]{2,1,0:T(8,128)}), f32[16,200,128]{2,1,0:T(8,128)S(1)}, u32[]{:S(2)}, u32[]{:S(2)}) %all-to-all-start.1) | async-done | bytes 1638432 | tf_op jit(solution)/shard_map/all_to_all | solution.py:409
  70.5 1.2 copy-done
  71.7 19.3 %shard_map.31 = (f32[512,512]{1,0:T(8,128)}, f32[512,512]{1,0:T(8,128)}, f32[512,512]{1,0:T(8,128)}) custom-call(f32[16,200,128]{2,1,0:T(8,128)} %copy-done, f32[512,512]{1,0:T(8,128)} %get-tuple-element.31.inverse0.inv0), custom_call_target="tpu_custom_call" | custom-call | tf_op jit(solution)/shard_map/pallas_call | solution.py:414
  91.0 0.0 all-gather.3.cloned.1.call-done
  91.1 8.4 %shard_map.32 = (bf16[2,768,512]{2,1,0:T(8,128)(2,1)}, bf16[2,768,512]{2,1,0:T(8,128)(2,1)}, f32[2,768,128]{2,1,0:T(8,128)}) custom-call(f32[4,2,6,128,128]{4,3,2,1,0:T(8,128)} %bitcast.8, s32[2,32,32]{2,1,0:T(8,128)} %pattern.3, f32[512,512]{1,0:T(8,128)} %get-tuple-element.31.inverse0.inv0, f32[512,512]{1,0:T(8,128)} %get-tuple-element.33.across, ...), custom_call_target="tpu_custom_call" | custom-call | tf_op jit(solution)/shard_map/pallas_call | solution.py:421
  99.4 0.0 collective-permute-done.2.ac2
  99.4 0.0 copy-start.2
  99.5 0.0 collective-permute-done.1.ac3
  99.5 0.0 collective-permute-done.ac1
  99.5 0.9 copy-done.2
  100.4 10.0 %shard_map.33 = f32[8,128,8,128]{3,2,1,0:T(8,128)} custom-call(f32[8,128,8,128]{3,2,1,0:T(8,128)} %bitcast.7, s32[2,32,32]{2,1,0:T(8,128)} %pattern.3, bf16[2,768,512]{2,1,0:T(8,128)(2,1)} %get-tuple-element.35.xh_in, bf16[2,768,512]{2,1,0:T(8,128)(2,1)} %get-tuple-element.36.xl_in, f32[2,768,128]{2,1,0:T(8,128)} %get-tuple-element.37.own_cols, ...), custom_call_target="tpu_custom_call" | custom-call | tf_op jit(solution)/shard_map/pallas_call | solution.py:428
  (2 shorter events, 0.0 us)
Async XLA Ops:
  6.5 84.5 %all-gather.3.cloned.1.call-start = ((), (), s32[]{:S(2)}) async-start(), calls=%async_computation.2 | async-start | bytes 3932160 | tf_op jit(solution)/shard_map/all_gather | solution.py:407
  9.2 2.7 %copy-start.3 = (f32[16,72,128]{2,1,0:T(8,128)S(1)}, f32[16,72,128]{2,1,0:T(8,128)}, u32[]{:S(2)}) copy-start(f32[16,72,128]{2,1,0:T(8,128)} %get-tuple-element.28) | copy-start | bytes 1769476
  29.2 22.7 %copy-start.1 = (f32[2,128,768]{2,1,0:T(8,128)S(1)}, f32[2,128,768]{2,1,0:T(8,128)}, u32[]{:S(2)}) copy-start(f32[2,128,768]{2,1,0:T(8,128)} %get-tuple-element.38.ac0) | copy-start | bytes 2359300
  29.2 41.3 %all-to-all-start.1 = ((f32[16,200,128]{2,1,0:T(8,128)}), f32[16,200,128]{2,1,0:T(8,128)S(1)}, u32[]{:S(2)}, u32[]{:S(2)}) async-start(f32[16,200,128]{2,1,0:T(8,128)} %get-tuple-element.32), calls=%async_computation.1 | async-start | bytes 3276800 | tf_op jit(solution)/shard_map/all_to_all | solution.py:409
  51.9 47.6 %collective-permute-start.2 = (f32[2,128,768]{2,1,0:T(8,128)S(1)}, f32[2,128,768]{2,1,0:T(8,128)S(1)}, u32[]{:S(2)}, u32[]{:S(2)}) collective-permute-start(f32[2,128,768]{2,1,0:T(8,128)S(1)} %copy-done.1), channel_id=1, source_target_pairs={{0,8},{4,12},{8,0},{12,4},{1,9},{5,13},{9,1},{13,5},{2,10},{6,14},... | collective-permute-start | bytes 2359304 | tf_op jit(solution)/shard_map/ppermute | solution.py:412
  55.0 44.5 %collective-permute-start.1 = (f32[2,128,768]{2,1,0:T(8,128)S(1)}, f32[2,128,768]{2,1,0:T(8,128)}, u32[]{:S(2)}, u32[]{:S(2)}) collective-permute-start(f32[2,128,768]{2,1,0:T(8,128)S(1)} %copy-done.1), channel_id=1, source_target_pairs={{0,12},{4,0},{8,4},{12,8},{1,13},{5,1},{9,5},{13,9},{2,14},{6,2},{... | collective-permute-start | bytes 2359304 | tf_op jit(solution)/shard_map/ppermute | solution.py:412
  56.1 43.4 %collective-permute-start = (f32[2,128,768]{2,1,0:T(8,128)S(1)}, f32[2,128,768]{2,1,0:T(8,128)}, u32[]{:S(2)}, u32[]{:S(2)}) collective-permute-start(f32[2,128,768]{2,1,0:T(8,128)S(1)} %copy-done.1), channel_id=1, source_target_pairs={{0,4},{4,8},{8,12},{12,0},{1,5},{5,9},{9,13},{13,1},{2,6},{6,10},{... | collective-permute-start | bytes 2359304 | tf_op jit(solution)/shard_map/ppermute | solution.py:412
  70.5 1.2 copy-start
  99.4 0.9 copy-start.2
Sparse Core Ops, SparseCore 0:
  11.9 60.3 all-gather.2
